TPU v7x, 512 devices: a whole 4x4x16 slice. The times are simulated.
512 devices in a mesh: outer: 32 (over y_lo, z), inner: 16 (over x, y_hi, core).
Axes of the slice: x: 4, y: 4 (y_hi: 2, y_lo: 2; y = y_hi * 2 + y_lo), z: 16, core: 2. Of those that a mesh axis runs over, the one named last changes fastest.
Arguments:
- queries: bfloat16 [262144, 1024], P(('outer', 'inner')), may hold values from -6 to 6
- keys: bfloat16 [262144, 128], P(('outer', 'inner')), may hold values from -6 to 6
- values: bfloat16 [262144, 128], P(('outer', 'inner')), may hold values from -6 to 6
- doc_lengths: int32 [64], replicated, may hold values from 1 to 32768, 262144 in all
Outputs:
- attended: bfloat16 [262144, 1024], P(('outer', 'inner'))
- log_total: float32 [8, 262144], P(None, ('outer', 'inner'))
Inputs may be any that keep to these rules, and one draw needn't show every extreme that they name: `doc_lengths`: the documents lie end to end from position 0 and fill the row; the longest has exactly 32768 positions.
All inputs are finite; a program needn't handle non-finite values.
Results may differ from a plain program's by a relative error of at most 0.0041.
Values may be sent and summed in bfloat16 or wider, within the bound.
No kernel may reach another device: no remote copies, remote signals or barrier semaphores. Data moves between devices by JAX's collectives and lax.ppermute only.
A program may use at most 64 MiB of HBM per device.

v0:
```python
from functools import reduce

import jax
import jax.numpy as jnp
from jax import lax
from jax.sharding import PartitionSpec as P

STEPS = 3


def from_behind(block, axis, distance):
    devices = range(lax.axis_size(axis))
    route = [(i - distance, i) for i in devices if i - distance in devices]
    return lax.ppermute(block, axis, route)


def from_behind_2(block, axis, distance):
    devices = range(lax.axis_size(axis))
    route = [((i - distance) % len(devices), i) for i in devices]
    return lax.ppermute(block, axis, route)


def shards(queries, keys, values, doc_lengths):
    tok_rows = keys.shape[0]
    head_size = keys.shape[1]
    head_count = queries.shape[1] // head_size
    n_inner = lax.axis_size("inner")
    outer_idx = lax.axis_index("outer")
    inner_idx = lax.axis_index("inner")
    itself = outer_idx * n_inner + inner_idx
    ends = jnp.cumsum(doc_lengths)
    offsets = jnp.arange(tok_rows, dtype=jnp.int32)
    reach = STEPS * tok_rows
    scale = head_size ** (-0.5)

    def place(device):
        where_at = device * tok_rows + offsets
        doc_of = jnp.sum((where_at[:, None] >= ends[None, :]).astype(jnp.int32), axis=1)
        return (where_at, doc_of)

    my_pos, my_doc = place(itself)
    near_list = []
    far_list = []
    far = from_behind((keys, values), "outer", 1)
    carried = (keys, values, far[0], far[1])
    for step in range(1, STEPS + 1):
        carried = from_behind_2((carried[0], carried[1], carried[2], carried[3]), "inner", 1)
        near_list.append((carried[0], carried[1]))
        far_list.append((carried[2], carried[3]))
    blocks = [(keys, values)]
    for step in range(1, STEPS + 1):
        inside = inner_idx >= step
        near = near_list[step - 1]
        remote = far_list[step - 1]
        blocks.append(
            (jnp.where(inside, near[0], remote[0]), jnp.where(inside, near[1], remote[1]))
        )
    masks = []
    for step in range(STEPS + 1):
        key_pos, key_doc = place(itself - step)
        gap = my_pos[:, None] - key_pos[None, :]
        masks.append(
            (key_pos[None, :] >= 0)
            & (gap >= 0)
            & (gap < reach)
            & (key_doc[None, :] == my_doc[:, None])
        )
    block_rows = 128
    block_count = tok_rows // block_rows
    flat_queries = queries.reshape(block_count, block_rows * head_count, head_size)
    mask_blocks = jnp.transpose(
        jnp.stack(masks).reshape(STEPS + 1, block_count, block_rows, tok_rows), (1, 0, 2, 3)
    )

    def score_block(query_rows, key_block, allowed):
        score = (
            jnp.einsum("rd,kd->rk", query_rows, key_block, preferred_element_type=jnp.float32)
            * scale
        )
        score = score.reshape(block_rows, head_count, tok_rows)
        return jnp.where(allowed[:, None, :], score, -jnp.inf)

    def weigh(weight_rows, value_block):
        return jnp.dot(weight_rows, value_block, preferred_element_type=jnp.float32)

    def query_block(inputs):
        query_rows, block_masks = inputs
        scores = []
        for index, block in enumerate(blocks):
            allowed = block_masks[index]
            piece = score_block(query_rows, block[0], allowed)
            scores.append(piece)
        top = reduce(jnp.maximum, [jnp.max(piece, axis=2) for piece in scores])
        total = jnp.zeros((block_rows, head_count), jnp.float32)
        numer = jnp.zeros((block_rows * head_count, head_size), jnp.float32)
        for index, block in enumerate(blocks):
            expon = jnp.exp(scores[index] - top[:, :, None])
            total = total + jnp.sum(expon, axis=2)
            weight_rows = expon.astype(jnp.bfloat16).reshape(block_rows * head_count, tok_rows)
            term = weigh(weight_rows, block[1])
            numer = numer + term
        outcome = (numer.reshape(block_rows, head_count, head_size) / total[:, :, None]).astype(
            jnp.bfloat16
        )
        return (outcome.reshape(block_rows, head_count * head_size), top + jnp.log(total))

    outcome, log_part = lax.map(query_block, (flat_queries, mask_blocks))
    attended = outcome.reshape(tok_rows, head_count * head_size)
    log_total = jnp.transpose(log_part.reshape(tok_rows, head_count))
    return (attended, log_total)


def solution(mesh):
    placed = (
        P(("outer", "inner"), None),
        P(("outer", "inner"), None),
        P(("outer", "inner"), None),
        P(),
    )
    return jax.shard_map(
        shards,
        mesh=mesh,
        in_specs=placed,
        out_specs=(P(("outer", "inner"), None), P(None, ("outer", "inner"))),
        check_vma=False,
    )
```

profile of v0, /device:TPU:72, one launch (start us, length us, event | category | flops | bytes accessed | tf_op | source)
XLA Modules:
  0.0 110.8 jit_solution(15139643183702878138)
XLA Ops:
  0.6 2.1 %collective-permute-start = (bf16[512,128]{1,0:T(8,128)(2,1)}, bf16[512,128]{1,0:T(8,128)(2,1)S(1)}, u32[]{:S(2)}, u32[]{:S(2)}) collective-permute-start(bf16[512,128]{1,0:T(8,128)(2,1)} %param.7), channel_id=1, source_target_pairs={{15,0},{0,1},{1,2},{2,3},{3,4},{4,5},{5,6},{6,7},{7,8},{8,9},{9,10... | collective-permute-start | bytes 393224 | tf_op jit(solution)/shard_map/ppermute | solution.py:20
  2.7 3.8 %collective-permute-start.1 = (bf16[512,128]{1,0:T(8,128)(2,1)}, bf16[512,128]{1,0:T(8,128)(2,1)S(1)}, u32[]{:S(2)}, u32[]{:S(2)}) collective-permute-start(bf16[512,128]{1,0:T(8,128)(2,1)} %param.7), channel_id=1, source_target_pairs={{0,16},{16,32},{32,48},{48,64},{64,80},{80,96},{96,112},{112,128},... | collective-permute-start | bytes 393224 | tf_op jit(solution)/shard_map/ppermute | solution.py:14
  6.5 4.0 %collective-permute-start.7 = (bf16[512,128]{1,0:T(8,128)(2,1)}, bf16[512,128]{1,0:T(8,128)(2,1)S(1)}, u32[]{:S(2)}, u32[]{:S(2)}) collective-permute-start(bf16[512,128]{1,0:T(8,128)(2,1)} %param.8), channel_id=1, source_target_pairs={{15,0},{0,1},{1,2},{2,3},{3,4},{4,5},{5,6},{6,7},{7,8},{8,9},{9,10... | collective-permute-start | bytes 393224 | tf_op jit(solution)/shard_map/ppermute | solution.py:20
  10.6 5.0 %collective-permute-start.8 = (bf16[512,128]{1,0:T(8,128)(2,1)}, bf16[512,128]{1,0:T(8,128)(2,1)S(1)}, u32[]{:S(2)}, u32[]{:S(2)}) collective-permute-start(bf16[512,128]{1,0:T(8,128)(2,1)} %param.8), channel_id=1, source_target_pairs={{0,16},{16,32},{32,48},{48,64},{64,80},{80,96},{96,112},{112,128},... | collective-permute-start | bytes 393224 | tf_op jit(solution)/shard_map/ppermute | solution.py:14
  15.7 0.7 copy.17
  16.8 1.8 %fusion.32 = (pred[1,4,128,512]{3,2,0,1:T(8,128)(4,1)S(1)}, pred[1,4,128,512]{3,2,0,1:T(8,128)(4,1)S(1)}, pred[1,4,128,512]{3,2,0,1:T(8,128)(4,1)S(1)}, pred[1,4,128,512]{3,2,0,1:T(8,128)(4,1)S(1)}) fusion(s32[4,128]{1,0:T(4,128)S(1)} %bitcast.79, s32[512]{0:T(512)S(1)} %get-tuple-element.79, s32[512]{0:T(512)S(1)} %get-tuple-element.131, ...), kind=kLoop, calls=%fused_computation.61 | loop fusion | flops 7340032 | bytes 1071104 | tf_op jit(solution)/shard_map/and | solution.py:63
  18.7 1.9 %collective-permute-start.3 = (bf16[512,128]{1,0:T(8,128)(2,1)S(1)}, bf16[512,128]{1,0:T(8,128)(2,1)S(1)}, u32[]{:S(2)}, u32[]{:S(2)}) collective-permute-start(bf16[512,128]{1,0:T(8,128)(2,1)S(1)} %collective-permute-done), channel_id=1, source_target_pairs={{15,0},{0,1},{1,2},{2,3},{3,4},{4,5},{5,6},{6,7},{7,8},{8,9},{9,10... | collective-permute-start | bytes 393224 | tf_op jit(solution)/shard_map/ppermute | solution.py:20
  20.6 4.2 %collective-permute-start.2 = (bf16[512,128]{1,0:T(8,128)(2,1)S(1)}, bf16[512,128]{1,0:T(8,128)(2,1)S(1)}, u32[]{:S(2)}, u32[]{:S(2)}) collective-permute-start(bf16[512,128]{1,0:T(8,128)(2,1)S(1)} %collective-permute-done.1), channel_id=1, source_target_pairs={{15,0},{0,1},{1,2},{2,3},{3,4},{4,5},{5,6},{6,7},{7,8},{8,9},{9,10... | collective-permute-start | bytes 393224 | tf_op jit(solution)/shard_map/ppermute | solution.py:20
  24.8 1.9 %collective-permute-start.10 = (bf16[512,128]{1,0:T(8,128)(2,1)S(1)}, bf16[512,128]{1,0:T(8,128)(2,1)S(1)}, u32[]{:S(2)}, u32[]{:S(2)}) collective-permute-start(bf16[512,128]{1,0:T(8,128)(2,1)S(1)} %collective-permute-done.7), channel_id=1, source_target_pairs={{15,0},{0,1},{1,2},{2,3},{3,4},{4,5},{5,6},{6,7},{7,8},{8,9},{9,10... | collective-permute-start | bytes 393224 | tf_op jit(solution)/shard_map/ppermute | solution.py:20
  26.7 1.4 %add_bitcast_fusion = pred[4,4,128,512]{3,2,1,0:T(8,128)(4,1)} fusion(pred[1,4,128,512]{3,2,0,1:T(8,128)(4,1)S(1)} %get-tuple-element.127, pred[1,4,128,512]{3,2,0,1:T(8,128)(4,1)S(1)} %get-tuple-element.126, pred[1,4,128,512]{3,2,0,1:T(8,128)(4,1)S(1)} %get-tuple-element.125, pred[1,4,128,512]{3,2,0,1:T(8,128)(4,1)S(1)} %get-tuple-element.124), kind=kLoop, calls=%fused_computation.50 | loop fusion | flops 3145728 | bytes 2097152 | tf_op jit(solution)/shard_map/transpose | solution.py:71
  28.6 4.3 %collective-permute-start.9 = (bf16[512,128]{1,0:T(8,128)(2,1)S(1)}, bf16[512,128]{1,0:T(8,128)(2,1)S(1)}, u32[]{:S(2)}, u32[]{:S(2)}) collective-permute-start(bf16[512,128]{1,0:T(8,128)(2,1)S(1)} %collective-permute-done.8), channel_id=1, source_target_pairs={{15,0},{0,1},{1,2},{2,3},{3,4},{4,5},{5,6},{6,7},{7,8},{8,9},{9,10... | collective-permute-start | bytes 393224 | tf_op jit(solution)/shard_map/ppermute | solution.py:20
  33.0 1.9 %collective-permute-start.5 = (bf16[512,128]{1,0:T(8,128)(2,1)S(1)}, bf16[512,128]{1,0:T(8,128)(2,1)S(1)}, u32[]{:S(2)}, u32[]{:S(2)}) collective-permute-start(bf16[512,128]{1,0:T(8,128)(2,1)S(1)} %collective-permute-done.3), channel_id=1, source_target_pairs={{15,0},{0,1},{1,2},{2,3},{3,4},{4,5},{5,6},{6,7},{7,8},{8,9},{9,10... | collective-permute-start | bytes 393224 | tf_op jit(solution)/shard_map/ppermute | solution.py:20
  34.9 4.2 %collective-permute-start.4 = (bf16[512,128]{1,0:T(8,128)(2,1)S(1)}, bf16[512,128]{1,0:T(8,128)(2,1)S(1)}, u32[]{:S(2)}, u32[]{:S(2)}) collective-permute-start(bf16[512,128]{1,0:T(8,128)(2,1)S(1)} %collective-permute-done.2), channel_id=1, source_target_pairs={{15,0},{0,1},{1,2},{2,3},{3,4},{4,5},{5,6},{6,7},{7,8},{8,9},{9,10... | collective-permute-start | bytes 393224 | tf_op jit(solution)/shard_map/ppermute | solution.py:20
  39.1 1.9 %collective-permute-start.12 = (bf16[512,128]{1,0:T(8,128)(2,1)S(1)}, bf16[512,128]{1,0:T(8,128)(2,1)S(1)}, u32[]{:S(2)}, u32[]{:S(2)}) collective-permute-start(bf16[512,128]{1,0:T(8,128)(2,1)S(1)} %collective-permute-done.10), channel_id=1, source_target_pairs={{15,0},{0,1},{1,2},{2,3},{3,4},{4,5},{5,6},{6,7},{7,8},{8,9},{9,10... | collective-permute-start | bytes 393224 | tf_op jit(solution)/shard_map/ppermute | solution.py:20
  41.0 4.3 %collective-permute-start.11 = (bf16[512,128]{1,0:T(8,128)(2,1)S(1)}, bf16[512,128]{1,0:T(8,128)(2,1)S(1)}, u32[]{:S(2)}, u32[]{:S(2)}) collective-permute-start(bf16[512,128]{1,0:T(8,128)(2,1)S(1)} %collective-permute-done.9), channel_id=1, source_target_pairs={{15,0},{0,1},{1,2},{2,3},{3,4},{4,5},{5,6},{6,7},{7,8},{8,9},{9,10... | collective-permute-start | bytes 393224 | tf_op jit(solution)/shard_map/ppermute | solution.py:20
  45.4 1.9 %collective-permute-start.6 = (bf16[512,128]{1,0:T(8,128)(2,1)S(1)}, bf16[512,128]{1,0:T(8,128)(2,1)S(1)}, u32[]{:S(2)}, u32[]{:S(2)}) collective-permute-start(bf16[512,128]{1,0:T(8,128)(2,1)S(1)} %collective-permute-done.4), channel_id=1, source_target_pairs={{15,0},{0,1},{1,2},{2,3},{3,4},{4,5},{5,6},{6,7},{7,8},{8,9},{9,10... | collective-permute-start | bytes 393224 | tf_op jit(solution)/shard_map/ppermute | solution.py:20
  47.4 3.6 %collective-permute-done.11 = bf16[512,128]{1,0:T(8,128)(2,1)S(1)} collective-permute-done((bf16[512,128]{1,0:T(8,128)(2,1)S(1)}, bf16[512,128]{1,0:T(8,128)(2,1)S(1)}, u32[]{:S(2)}, u32[]{:S(2)}) %collective-permute-start.11) | collective-permute-done | bytes 131104 | tf_op jit(solution)/shard_map/ppermute | solution.py:20
  51.0 2.1 %collective-permute-start.13 = (bf16[512,128]{1,0:T(8,128)(2,1)S(1)}, bf16[512,128]{1,0:T(8,128)(2,1)S(1)}, u32[]{:S(2)}, u32[]{:S(2)}) collective-permute-start(bf16[512,128]{1,0:T(8,128)(2,1)S(1)} %collective-permute-done.11), channel_id=1, source_target_pairs={{15,0},{0,1},{1,2},{2,3},{3,4},{4,5},{5,6},{6,7},{7,8},{8,9},{9,10... | collective-permute-start | bytes 393224 | tf_op jit(solution)/shard_map/ppermute | solution.py:20
  53.1 2.2 %collective-permute-done.6 = bf16[512,128]{1,0:T(8,128)(2,1)S(1)} collective-permute-done((bf16[512,128]{1,0:T(8,128)(2,1)S(1)}, bf16[512,128]{1,0:T(8,128)(2,1)S(1)}, u32[]{:S(2)}, u32[]{:S(2)}) %collective-permute-start.6) | collective-permute-done | bytes 131104 | tf_op jit(solution)/shard_map/ppermute | solution.py:20
  55.3 5.5 %collective-permute-done.13 = bf16[512,128]{1,0:T(8,128)(2,1)S(1)} collective-permute-done((bf16[512,128]{1,0:T(8,128)(2,1)S(1)}, bf16[512,128]{1,0:T(8,128)(2,1)S(1)}, u32[]{:S(2)}, u32[]{:S(2)}) %collective-permute-start.13) | collective-permute-done | bytes 131104 | tf_op jit(solution)/shard_map/ppermute | solution.py:20
  60.9 49.3 %while.12 = (s32[]{:T(128)}, bf16[4,128,1024]{2,1,0:T(8,128)(2,1)}, f32[4,128,8]{1,2,0:T(8,128)S(1)}, pred[4,4,128,512]{3,2,1,0:T(8,128)(4,1)}, bf16[4,1024,128]...) while((s32[]{:T(128)}, bf16[4,128,1024]{2,1,0:T(8,128)(2,1)}, ...), condition=%wide.region_14.15_spmd, body=%wide.region_5.14_spmd.sunk | while | flops 1089076224 | bytes 44179704 | solution.py:107
  60.9 1.0 dynamic-slice_bitcast_fusion.5
  61.8 0.6 broadcast_bitcast_fusion.6
  62.5 0.6 copy.26
  63.1 0.6 copy.29
  63.7 0.6 broadcast_bitcast_fusion.7
  64.3 0.6 copy.27
  65.0 0.6 copy.28
  67.7 1.1 %fusion.90 = (f32[1024]{0:T(1024)S(1)}, f32[1024]{0:T(1024)S(1)}, f32[1024]{0:T(1024)S(1)}, f32[1024]{0:T(1024)S(1)}) fusion(f32[1024,512]{0,1:T(8,128)S(1)} %get-tuple-element.250, f32[1024]{0:T(1024)S(1)} %maximum_maximum_fusion.2, f32[1024,512]{0,1:T(8,128)S(1)} %get-tuple-element.240, f32[1024,512]{0,1:T(8,128)S(1)} %get-tuple-element.251, ...), kind=kLoop, calls=%fused_computation.10.clone.1 | loop fusion | flops 4190208 | bytes 8409088 | tf_op jit(solution)/shard_map/while/body/eval_jaxpr/reduce_sum | solution.py:98
  68.8 1.4 %fusion.89 = f32[1024,128]{1,0:T(8,128)S(1)} fusion(bf16[512,128]{1,0:T(8,128)(2,1)} %get-tuple-element.304, f32[1024,512]{0,1:T(8,128)S(1)} %get-tuple-element.240, f32[1024]{0:T(1024)S(1)} %maximum_maximum_fusion.2), kind=kOutput, calls=%fused_computation.19.clone.1 | convolution fusion | flops 135266304 | bytes 2756608 | tf_op jit(solution)/shard_map/while/body/eval_jaxpr/dot_general | solution.py:84
  72.4 0.8 fusion.91
  73.2 1.0 dynamic-slice_bitcast_fusion.5
  74.2 0.6 broadcast_bitcast_fusion.6
  74.8 0.6 copy.26
  75.4 0.6 copy.29
  76.0 0.6 broadcast_bitcast_fusion.7
  76.7 0.6 copy.27
  77.3 0.6 copy.28
  79.0 0.5 fusion.88
  80.0 1.1 %fusion.90 = (f32[1024]{0:T(1024)S(1)}, f32[1024]{0:T(1024)S(1)}, f32[1024]{0:T(1024)S(1)}, f32[1024]{0:T(1024)S(1)}) fusion(f32[1024,512]{0,1:T(8,128)S(1)} %get-tuple-element.250, f32[1024]{0:T(1024)S(1)} %maximum_maximum_fusion.2, f32[1024,512]{0,1:T(8,128)S(1)} %get-tuple-element.240, f32[1024,512]{0,1:T(8,128)S(1)} %get-tuple-element.251, ...), kind=kLoop, calls=%fused_computation.10.clone.1 | loop fusion | flops 4190208 | bytes 8409088 | tf_op jit(solution)/shard_map/while/body/eval_jaxpr/reduce_sum | solution.py:98
  81.2 1.4 %fusion.89 = f32[1024,128]{1,0:T(8,128)S(1)} fusion(bf16[512,128]{1,0:T(8,128)(2,1)} %get-tuple-element.304, f32[1024,512]{0,1:T(8,128)S(1)} %get-tuple-element.240, f32[1024]{0:T(1024)S(1)} %maximum_maximum_fusion.2), kind=kOutput, calls=%fused_computation.19.clone.1 | convolution fusion | flops 135266304 | bytes 2756608 | tf_op jit(solution)/shard_map/while/body/eval_jaxpr/dot_general | solution.py:84
  84.7 0.8 fusion.91
  85.5 1.0 dynamic-slice_bitcast_fusion.5
  86.5 0.6 broadcast_bitcast_fusion.6
  87.1 0.6 copy.26
  87.7 0.6 copy.29
  88.4 0.6 broadcast_bitcast_fusion.7
  89.0 0.6 copy.27
  89.6 0.6 copy.28
  91.3 0.5 fusion.88
  92.3 1.1 %fusion.90 = (f32[1024]{0:T(1024)S(1)}, f32[1024]{0:T(1024)S(1)}, f32[1024]{0:T(1024)S(1)}, f32[1024]{0:T(1024)S(1)}) fusion(f32[1024,512]{0,1:T(8,128)S(1)} %get-tuple-element.250, f32[1024]{0:T(1024)S(1)} %maximum_maximum_fusion.2, f32[1024,512]{0,1:T(8,128)S(1)} %get-tuple-element.240, f32[1024,512]{0,1:T(8,128)S(1)} %get-tuple-element.251, ...), kind=kLoop, calls=%fused_computation.10.clone.1 | loop fusion | flops 4190208 | bytes 8409088 | tf_op jit(solution)/shard_map/while/body/eval_jaxpr/reduce_sum | solution.py:98
  93.5 1.4 %fusion.89 = f32[1024,128]{1,0:T(8,128)S(1)} fusion(bf16[512,128]{1,0:T(8,128)(2,1)} %get-tuple-element.304, f32[1024,512]{0,1:T(8,128)S(1)} %get-tuple-element.240, f32[1024]{0:T(1024)S(1)} %maximum_maximum_fusion.2), kind=kOutput, calls=%fused_computation.19.clone.1 | convolution fusion | flops 135266304 | bytes 2756608 | tf_op jit(solution)/shard_map/while/body/eval_jaxpr/dot_general | solution.py:84
  97.1 0.8 fusion.91
  97.8 1.0 dynamic-slice_bitcast_fusion.5
  98.8 0.6 broadcast_bitcast_fusion.6
  99.4 0.6 copy.26
  100.1 0.6 copy.29
  100.7 0.6 broadcast_bitcast_fusion.7
  101.3 0.6 copy.27
  101.9 0.6 copy.28
  104.7 1.1 %fusion.90 = (f32[1024]{0:T(1024)S(1)}, f32[1024]{0:T(1024)S(1)}, f32[1024]{0:T(1024)S(1)}, f32[1024]{0:T(1024)S(1)}) fusion(f32[1024,512]{0,1:T(8,128)S(1)} %get-tuple-element.250, f32[1024]{0:T(1024)S(1)} %maximum_maximum_fusion.2, f32[1024,512]{0,1:T(8,128)S(1)} %get-tuple-element.240, f32[1024,512]{0,1:T(8,128)S(1)} %get-tuple-element.251, ...), kind=kLoop, calls=%fused_computation.10.clone.1 | loop fusion | flops 4190208 | bytes 8409088 | tf_op jit(solution)/shard_map/while/body/eval_jaxpr/reduce_sum | solution.py:98
  105.8 1.4 %fusion.89 = f32[1024,128]{1,0:T(8,128)S(1)} fusion(bf16[512,128]{1,0:T(8,128)(2,1)} %get-tuple-element.304, f32[1024,512]{0,1:T(8,128)S(1)} %get-tuple-element.240, f32[1024]{0:T(1024)S(1)} %maximum_maximum_fusion.2), kind=kOutput, calls=%fused_computation.19.clone.1 | convolution fusion | flops 135266304 | bytes 2756608 | tf_op jit(solution)/shard_map/while/body/eval_jaxpr/dot_general | solution.py:84
  109.4 0.8 fusion.91
  110.2 0.6 copy-done.2
  (95 shorter events, 16.7 us)
Async XLA Ops:
  0.6 27.5 %copy-start.1 = (bf16[512,1024]{1,0:T(8,128)(2,1)S(1)}, bf16[512,1024]{1,0:T(8,128)(2,1)}, u32[]{:S(2)}) copy-start(bf16[512,1024]{1,0:T(8,128)(2,1)} %param.6) | copy-start | bytes 3145732
  0.6 18.0 %collective-permute-start = (bf16[512,128]{1,0:T(8,128)(2,1)}, bf16[512,128]{1,0:T(8,128)(2,1)S(1)}, u32[]{:S(2)}, u32[]{:S(2)}) collective-permute-start(bf16[512,128]{1,0:T(8,128)(2,1)} %param.7), channel_id=1, source_target_pairs={{15,0},{0,1},{1,2},{2,3},{3,4},{4,5},{5,6},{6,7},{7,8},{8,9},{9,10... | collective-permute-start | bytes 393224 | tf_op jit(solution)/shard_map/ppermute | solution.py:20
  2.7 17.9 %collective-permute-start.1 = (bf16[512,128]{1,0:T(8,128)(2,1)}, bf16[512,128]{1,0:T(8,128)(2,1)S(1)}, u32[]{:S(2)}, u32[]{:S(2)}) collective-permute-start(bf16[512,128]{1,0:T(8,128)(2,1)} %param.7), channel_id=1, source_target_pairs={{0,16},{16,32},{32,48},{48,64},{64,80},{80,96},{96,112},{112,128},... | collective-permute-start | bytes 393224 | tf_op jit(solution)/shard_map/ppermute | solution.py:14
  6.5 18.3 %collective-permute-start.7 = (bf16[512,128]{1,0:T(8,128)(2,1)}, bf16[512,128]{1,0:T(8,128)(2,1)S(1)}, u32[]{:S(2)}, u32[]{:S(2)}) collective-permute-start(bf16[512,128]{1,0:T(8,128)(2,1)} %param.8), channel_id=1, source_target_pairs={{15,0},{0,1},{1,2},{2,3},{3,4},{4,5},{5,6},{6,7},{7,8},{8,9},{9,10... | collective-permute-start | bytes 393224 | tf_op jit(solution)/shard_map/ppermute | solution.py:20
  10.6 18.0 %collective-permute-start.8 = (bf16[512,128]{1,0:T(8,128)(2,1)}, bf16[512,128]{1,0:T(8,128)(2,1)S(1)}, u32[]{:S(2)}, u32[]{:S(2)}) collective-permute-start(bf16[512,128]{1,0:T(8,128)(2,1)} %param.8), channel_id=1, source_target_pairs={{0,16},{16,32},{32,48},{48,64},{64,80},{80,96},{96,112},{112,128},... | collective-permute-start | bytes 393224 | tf_op jit(solution)/shard_map/ppermute | solution.py:14
  18.7 14.3 %collective-permute-start.3 = (bf16[512,128]{1,0:T(8,128)(2,1)S(1)}, bf16[512,128]{1,0:T(8,128)(2,1)S(1)}, u32[]{:S(2)}, u32[]{:S(2)}) collective-permute-start(bf16[512,128]{1,0:T(8,128)(2,1)S(1)} %collective-permute-done), channel_id=1, source_target_pairs={{15,0},{0,1},{1,2},{2,3},{3,4},{4,5},{5,6},{6,7},{7,8},{8,9},{9,10... | collective-permute-start | bytes 393224 | tf_op jit(solution)/shard_map/ppermute | solution.py:20
  20.6 14.3 %collective-permute-start.2 = (bf16[512,128]{1,0:T(8,128)(2,1)S(1)}, bf16[512,128]{1,0:T(8,128)(2,1)S(1)}, u32[]{:S(2)}, u32[]{:S(2)}) collective-permute-start(bf16[512,128]{1,0:T(8,128)(2,1)S(1)} %collective-permute-done.1), channel_id=1, source_target_pairs={{15,0},{0,1},{1,2},{2,3},{3,4},{4,5},{5,6},{6,7},{7,8},{8,9},{9,10... | collective-permute-start | bytes 393224 | tf_op jit(solution)/shard_map/ppermute | solution.py:20
  24.8 14.3 %collective-permute-start.10 = (bf16[512,128]{1,0:T(8,128)(2,1)S(1)}, bf16[512,128]{1,0:T(8,128)(2,1)S(1)}, u32[]{:S(2)}, u32[]{:S(2)}) collective-permute-start(bf16[512,128]{1,0:T(8,128)(2,1)S(1)} %collective-permute-done.7), channel_id=1, source_target_pairs={{15,0},{0,1},{1,2},{2,3},{3,4},{4,5},{5,6},{6,7},{7,8},{8,9},{9,10... | collective-permute-start | bytes 393224 | tf_op jit(solution)/shard_map/ppermute | solution.py:20
  28.1 32.7 %copy-start = (bf16[512,128]{1,0:T(8,128)(2,1)S(1)}, bf16[512,128]{1,0:T(8,128)(2,1)}, u32[]{:S(2)}) copy-start(bf16[512,128]{1,0:T(8,128)(2,1)} %param.7) | copy-start | bytes 393220
  28.6 12.4 %collective-permute-start.9 = (bf16[512,128]{1,0:T(8,128)(2,1)S(1)}, bf16[512,128]{1,0:T(8,128)(2,1)S(1)}, u32[]{:S(2)}, u32[]{:S(2)}) collective-permute-start(bf16[512,128]{1,0:T(8,128)(2,1)S(1)} %collective-permute-done.8), channel_id=1, source_target_pairs={{15,0},{0,1},{1,2},{2,3},{3,4},{4,5},{5,6},{6,7},{7,8},{8,9},{9,10... | collective-permute-start | bytes 393224 | tf_op jit(solution)/shard_map/ppermute | solution.py:20
  33.0 20.1 %collective-permute-start.5 = (bf16[512,128]{1,0:T(8,128)(2,1)S(1)}, bf16[512,128]{1,0:T(8,128)(2,1)S(1)}, u32[]{:S(2)}, u32[]{:S(2)}) collective-permute-start(bf16[512,128]{1,0:T(8,128)(2,1)S(1)} %collective-permute-done.3), channel_id=1, source_target_pairs={{15,0},{0,1},{1,2},{2,3},{3,4},{4,5},{5,6},{6,7},{7,8},{8,9},{9,10... | collective-permute-start | bytes 393224 | tf_op jit(solution)/shard_map/ppermute | solution.py:20
  34.9 10.5 %collective-permute-start.4 = (bf16[512,128]{1,0:T(8,128)(2,1)S(1)}, bf16[512,128]{1,0:T(8,128)(2,1)S(1)}, u32[]{:S(2)}, u32[]{:S(2)}) collective-permute-start(bf16[512,128]{1,0:T(8,128)(2,1)S(1)} %collective-permute-done.2), channel_id=1, source_target_pairs={{15,0},{0,1},{1,2},{2,3},{3,4},{4,5},{5,6},{6,7},{7,8},{8,9},{9,10... | collective-permute-start | bytes 393224 | tf_op jit(solution)/shard_map/ppermute | solution.py:20
  39.1 16.2 %collective-permute-start.12 = (bf16[512,128]{1,0:T(8,128)(2,1)S(1)}, bf16[512,128]{1,0:T(8,128)(2,1)S(1)}, u32[]{:S(2)}, u32[]{:S(2)}) collective-permute-start(bf16[512,128]{1,0:T(8,128)(2,1)S(1)} %collective-permute-done.10), channel_id=1, source_target_pairs={{15,0},{0,1},{1,2},{2,3},{3,4},{4,5},{5,6},{6,7},{7,8},{8,9},{9,10... | collective-permute-start | bytes 393224 | tf_op jit(solution)/shard_map/ppermute | solution.py:20
  41.0 9.9 %collective-permute-start.11 = (bf16[512,128]{1,0:T(8,128)(2,1)S(1)}, bf16[512,128]{1,0:T(8,128)(2,1)S(1)}, u32[]{:S(2)}, u32[]{:S(2)}) collective-permute-start(bf16[512,128]{1,0:T(8,128)(2,1)S(1)} %collective-permute-done.9), channel_id=1, source_target_pairs={{15,0},{0,1},{1,2},{2,3},{3,4},{4,5},{5,6},{6,7},{7,8},{8,9},{9,10... | collective-permute-start | bytes 393224 | tf_op jit(solution)/shard_map/ppermute | solution.py:20
  45.4 9.9 %collective-permute-start.6 = (bf16[512,128]{1,0:T(8,128)(2,1)S(1)}, bf16[512,128]{1,0:T(8,128)(2,1)S(1)}, u32[]{:S(2)}, u32[]{:S(2)}) collective-permute-start(bf16[512,128]{1,0:T(8,128)(2,1)S(1)} %collective-permute-done.4), channel_id=1, source_target_pairs={{15,0},{0,1},{1,2},{2,3},{3,4},{4,5},{5,6},{6,7},{7,8},{8,9},{9,10... | collective-permute-start | bytes 393224 | tf_op jit(solution)/shard_map/ppermute | solution.py:20
  51.0 9.9 %collective-permute-start.13 = (bf16[512,128]{1,0:T(8,128)(2,1)S(1)}, bf16[512,128]{1,0:T(8,128)(2,1)S(1)}, u32[]{:S(2)}, u32[]{:S(2)}) collective-permute-start(bf16[512,128]{1,0:T(8,128)(2,1)S(1)} %collective-permute-done.11), channel_id=1, source_target_pairs={{15,0},{0,1},{1,2},{2,3},{3,4},{4,5},{5,6},{6,7},{7,8},{8,9},{9,10... | collective-permute-start | bytes 393224 | tf_op jit(solution)/shard_map/ppermute | solution.py:20
  110.2 0.6 copy-start.2
where the time goes:
time: 112 us; the launch traced here: 111 us
  starting transfers between devices  43.6 us (39%)
  local copies, waits for them, and re-layouts  22.9 us (20%)
  matrix products  19.9 us (18%)
  other arithmetic  11.5 us (10%)
  waiting for transfers between devices  11.4 us (10%)
    ppermute x12, starting transfers between devices, from_behind_2(): return lax.ppermute(block, axis, route)  34.7 us
    broadcast_in_dim x28, local copies, waits for them, and re-layouts, score_block(): return jnp.where(allowed[:, None, :], score, -jnp.inf)  18.7 us
    dot_general x16, matrix products, weigh(): return jnp.dot(weight_rows, value_block, preferred_element_type=jnp.float32)  11.7 us
    ppermute x12, waiting for transfers between devices, from_behind_2(): return lax.ppermute(block, axis, route)  11.3 us
    ppermute x2, starting transfers between devices, from_behind(): return lax.ppermute(block, axis, route)  8.87 us
    dot_general x16, matrix products, score_block(): jnp.einsum('rd,kd->rk', query_rows, key_block, preferred_element_type=jnp...  8.22 us
    reduce_sum x4, other arithmetic, query_block(): total = total + jnp.sum(expon, axis=2)  4.49 us
    dynamic_update_slice x4, other arithmetic, shards(): outcome, log_part = lax.map(query_block, (flat_queries, mask_blocks))  3.16 us
  transfers between devices with their start and end apart: 14, of which 3 were waited for; matrix products, arithmetic and copies ran while one was open for 4% of the time, Pallas kernels for 0%

commit v1 on v0

v1 whole, which is shorter than its diff:
```python
import functools
import math

import jax
import jax.numpy as jnp
from jax import lax
from jax.experimental import pallas as pl
from jax.experimental.pallas import tpu as pltpu
from jax.sharding import PartitionSpec as P

AXES = ("outer", "inner")
LANES = 128
FAR = 2.0**15
NEG = -2.0**20
TILE = 128
HEADS_AT_ONCE = 2


def _inside(bounds, rows, offset, shape):
    at = lax.broadcasted_iota(jnp.int32, (rows, LANES), 0) + offset
    return (at >= bounds[0:1, :]) & (at < bounds[1:2, :])


def _dot_t(a, b):
    return lax.dot_general(a, b, (((1,), (1,)), ((), ())), preferred_element_type=jnp.float32)


def _stage(pieces, opens, closes, heads_here, scale, *refs):
    refs = list(refs)
    parity, bounds, q_ref = refs[:3]
    refs = refs[3:]
    rows = q_ref.shape[0]
    size = LANES
    n_blocks = len(pieces["steps"])
    kv = refs[:n_blocks]
    refs = refs[n_blocks:]
    if not opens:
        num_in, log_in = refs[:2]
        refs = refs[2:]
    num_out, log_out, key_s, val_s, doc_s = refs
    step = pl.program_id(0)

    @pl.when(step == 0)
    def _():
        b = bounds[...]
        mine = _inside(b, rows, 0, None)
        doc_s[...] = jnp.where(mine, -FAR, 0.0).astype(jnp.bfloat16)
        even = parity[0] == 0
        for n, back in enumerate(pieces["steps"]):
            here = pl.ds(n * rows, rows)
            if n_blocks == 2:
                one, two = kv[n], kv[1 - n]
                block = jnp.where(even, one[...], two[...])
            else:
                block = kv[n][...]
            key_s[here, 0:size] = block[0:rows]
            val_s[here, :] = block[rows : 2 * rows]
            theirs = _inside(b, rows, -back * rows, None)
            key_s[here, size : 2 * size] = jnp.where(theirs, 0.0, 1.0).astype(jnp.bfloat16)
        log_out[...] = jnp.zeros_like(log_out)

    tri = lax.broadcasted_iota(jnp.int32, (TILE, TILE), 0) - lax.broadcasted_iota(jnp.int32, (TILE, TILE), 1)
    lane = lax.broadcasted_iota(jnp.int32, (TILE, LANES), 1)

    def scores(i):
        rs = slice(i * TILE, (i + 1) * TILE)
        docs = doc_s[rs, :]
        left = jnp.concatenate(
            [
                jnp.concatenate([q_ref[rs, h * size : (h + 1) * size], docs], axis=1)
                for h in range(heads_here)
            ],
            axis=0,
        )
        start, count, _ = pieces["tiles"][i]
        return _dot_t(left, key_s[start : start + count, :])

    def finish(i, score):
        rs = slice(i * TILE, (i + 1) * TILE)
        start, count, edge = pieces["tiles"][i]
        out = []
        score = score.reshape(heads_here, TILE, count)
        if edge is not None:
            at, upper = edge
            keep = tri < 0 if upper else tri >= 0
            part = jnp.where(keep[None], score[:, :, at : at + TILE], NEG)
            parts = []
            if at:
                parts.append(score[:, :, :at])
            parts.append(part)
            if at + TILE < count:
                parts.append(score[:, :, at + TILE :])
            score = jnp.concatenate(parts, axis=2) if len(parts) > 1 else part
        top = jnp.max(score, axis=2, keepdims=True) * scale
        if not opens:
            logs = log_in[rs, :]
            before = jnp.stack(
                [
                    jnp.sum(jnp.where(lane == step * heads_here + h, logs, 0.0), axis=1, keepdims=True)
                    for h in range(heads_here)
                ]
            )
            top = jnp.maximum(top, before)
        expon = jnp.exp2(score * scale - top)
        total = jnp.sum(expon, axis=2, keepdims=True)
        weight = expon.astype(jnp.bfloat16).reshape(heads_here * TILE, count)
        num = jnp.dot(weight, val_s[start : start + count, :], preferred_element_type=jnp.float32)
        num = num.reshape(heads_here, TILE, size)
        if not opens:
            share = jnp.exp2(before - top)
            total = total + share
            for h in range(heads_here):
                out.append(num[h] + share[h] * num_in[rs, h * size : (h + 1) * size])
        else:
            out = [num[h] for h in range(heads_here)]
        inverse = 1.0 / total
        logs = top + jnp.log2(total)
        new = log_out[rs, :]
        for h in range(heads_here):
            num_out[rs, h * size : (h + 1) * size] = (out[h] * inverse[h]).astype(num_out.dtype)
            new = jnp.where(lane == step * heads_here + h, logs[h], new)
        log_out[rs, :] = new

    n = rows // TILE
    score = scores(0)
    for i in range(n):
        following = scores(i + 1) if i + 1 < n else None
        finish(i, score)
        score = following


def _call(name, pieces, parity, bounds, queries, kv, state, out_type):
    rows, width = queries.shape
    heads = width // LANES
    here = min(HEADS_AT_ONCE, heads)
    opens, closes = state is None, out_type == jnp.bfloat16
    scale = LANES**-0.5 * math.log2(math.e)
    whole = lambda x: pl.BlockSpec(x.shape, lambda s: (0, 0))
    wide = pl.BlockSpec((rows, here * LANES), lambda s: (0, s))
    logs = pl.BlockSpec((rows, LANES), lambda s: (0, 0))
    n = len(kv)
    count = sum(t[1] for t in pieces["tiles"]) * TILE * heads
    return pl.pallas_call(
        functools.partial(_stage, pieces, opens, closes, here, scale),
        grid=(heads // here,),
        in_specs=[pl.BlockSpec(memory_space=pltpu.SMEM), whole(bounds), wide]
        + [whole(x) for x in kv]
        + ([] if opens else [wide, logs]),
        out_specs=[wide, logs],
        out_shape=[
            jax.ShapeDtypeStruct((rows, width), out_type),
            jax.ShapeDtypeStruct((rows, LANES), jnp.float32),
        ],
        scratch_shapes=[
            pltpu.VMEM((n * rows, 2 * LANES), jnp.bfloat16),
            pltpu.VMEM((n * rows, LANES), jnp.bfloat16),
            pltpu.VMEM((rows, LANES), jnp.bfloat16),
        ],
        compiler_params=pltpu.CompilerParams(
            dimension_semantics=("arbitrary",), vmem_limit_bytes=48 * 1024 * 1024
        ),
        cost_estimate=pl.CostEstimate(
            flops=4 * count * LANES, bytes_accessed=6 * rows * width, transcendentals=count
        ),
        name=name,
    )(parity, bounds, queries, *kv, *(state or ()))


def shards(queries, keys, values, doc_lengths):
    rows = keys.shape[0]
    count = lax.axis_size("outer") * lax.axis_size("inner")
    me = lax.axis_index("outer") * lax.axis_size("inner") + lax.axis_index("inner")
    parity = (me % 2).astype(jnp.int32).reshape(1)
    n_docs = doc_lengths.shape[0]
    order = jnp.arange(n_docs)
    before = jnp.where(order[:, None] < jnp.arange(LANES)[None, :], doc_lengths[:, None], 0)
    starts = jnp.sum(before, axis=0)
    upto = jnp.where(order[:, None] <= jnp.arange(LANES)[None, :], doc_lengths[:, None], 0)
    ends = jnp.sum(upto, axis=0)
    bounds = jnp.concatenate([starts[None], ends[None]]).astype(jnp.int32) - me * rows

    def send(block, step_of):
        return lax.ppermute(
            block, AXES, [(i, i + step_of(i)) for i in range(count) if i + step_of(i) < count]
        )

    kv = jnp.concatenate([keys, values], axis=0)
    first = send(kv, lambda i: 1 if i % 2 else 3)
    second = send(kv, lambda i: 3 if i % 2 else 1)
    middle = send(first, lambda i: -1 if i % 2 else 1)

    n = rows // TILE
    own = {"steps": (0,), "tiles": [(0, (i + 1) * TILE, (i * TILE, False)) for i in range(n)]}
    sides = {"steps": (1, 3), "tiles": [(0, 0, None)] * n}
    sides = {
        "steps": (3, 1),
        "tiles": [(i * TILE, 2 * rows - i * TILE, (0, True)) for i in range(n)],
    }
    mid = {"steps": (2,), "tiles": [(0, rows, None)] * n}
    state = _call("own", own, parity, bounds, queries, [kv], None, jnp.float32)
    state = _call("sides", sides, parity, bounds, queries, [second, first], state, jnp.float32)
    attended, logs = _call("middle", mid, parity, bounds, queries, [middle], state, jnp.bfloat16)
    log_total = jnp.transpose(logs[:, : queries.shape[1] // LANES]) * math.log(2.0)
    return attended, log_total


def solution(mesh):
    placed = (P(AXES, None), P(AXES, None), P(AXES, None), P())
    return jax.shard_map(
        shards,
        mesh=mesh,
        in_specs=placed,
        out_specs=(P(AXES, None), P(None, AXES)),
        check_vma=False,
    )
```

time: 112 us -> 55.9 us (0.50)
  the two profiles are of different devices: /device:TPU:72 before, /device:TPU:8 now
where the time goes in v1:
time: 55.9 us; the launch traced here: 55.5 us
  Pallas kernels  25.9 us (46%)
  waiting for transfers between devices  13.1 us (23%)
  starting transfers between devices  9.9 us (18%)
  local copies, waits for them, and re-layouts  5.09 us (9%)
  other arithmetic  0.79 us (1%)
  between operations  0.73 us (1%)
    pallas_call x3, Pallas kernels, _call(): pl.pallas_call(functools.partial(_stage, pieces, opens, closes, here, sca...  25.9 us
    ppermute x3, waiting for transfers between devices, send(): lax.ppermute(block, AXES, [(i, i + step_of(i)) for i in range(count) if i...  13.1 us
    ppermute x3, starting transfers between devices, send(): lax.ppermute(block, AXES, [(i, i + step_of(i)) for i in range(count) if i...  9.9 us
    unnamed x6, local copies, waits for them, and re-layouts  4.17 us
  transfers between devices with their start and end apart: 3, of which 1 were waited for; matrix products, arithmetic and copies ran while one was open for 1% of the time, Pallas kernels for 27%

profile of v1, /device:TPU:8, one launch (start us, length us, event | category | flops | bytes accessed | tf_op | source)
XLA Modules:
  0.0 55.5 jit_solution(7465430740145375606)
XLA Ops:
  0.6 0.9 %constant_dynamic-update-slice_fusion.1 = bf16[1024,128]{1,0:T(8,128)(2,1)S(1)} fusion(bf16[512,128]{1,0:T(8,128)(2,1)} %param.5), kind=kLoop, calls=%fused_computation.6 | loop fusion | bytes 262144
  1.5 0.9 %constant_dynamic-update-slice_fusion.refs_3_ = bf16[1024,128]{1,0:T(8,128)(2,1)S(1)} fusion(bf16[1024,128]{1,0:T(8,128)(2,1)S(1)} %constant_dynamic-update-slice_fusion.1, bf16[512,128]{1,0:T(8,128)(2,1)} %param.6), kind=kLoop, calls=%fused_computation.5 | loop fusion | bytes 262144 | tf_op jit(solution)/shard_map/concatenate | solution.py:187
  2.5 3.6 %collective-permute-start = (bf16[1024,128]{1,0:T(8,128)(2,1)S(1)}, bf16[1024,128]{1,0:T(8,128)(2,1)S(1)}, u32[]{:S(2)}, u32[]{:S(2)}) collective-permute-start(bf16[1024,128]{1,0:T(8,128)(2,1)S(1)} %constant_dynamic-update-slice_fusion.refs_3_), channel_id=1, source_target_pairs={{0,3},{1,2},{2,5},{3,4},{4,7},{5,6},{6,9},{7,8},{8,11},{9,10},{10,... | collective-permute-start | bytes 786440 | tf_op jit(solution)/shard_map/ppermute | solution.py:183
  6.1 2.6 %collective-permute-start.2 = (bf16[1024,128]{1,0:T(8,128)(2,1)S(1)}, bf16[1024,128]{1,0:T(8,128)(2,1)S(1)}, u32[]{:S(2)}, u32[]{:S(2)}) collective-permute-start(bf16[1024,128]{1,0:T(8,128)(2,1)S(1)} %constant_dynamic-update-slice_fusion.refs_3_), channel_id=1, source_target_pairs={{0,1},{1,4},{2,3},{3,6},{4,5},{5,8},{6,7},{7,10},{8,9},{9,12},{10,... | collective-permute-start | bytes 786440 | tf_op jit(solution)/shard_map/ppermute | solution.py:183
  8.7 0.7 %select_reduce_fusion.1 = (s32[128]{0:T(128)S(1)}, s32[128]{0:T(128)S(1)}) fusion(s32[64]{0:T(128)} %param.7), kind=kLoop, calls=%fused_computation.3 | loop fusion | flops 48896 | bytes 1280 | tf_op jit(solution)/shard_map/reduce_sum | solution.py:177
  9.5 13.1 %collective-permute-done.refs_4_ = bf16[1024,128]{1,0:T(8,128)(2,1)S(1)} collective-permute-done((bf16[1024,128]{1,0:T(8,128)(2,1)S(1)}, bf16[1024,128]{1,0:T(8,128)(2,1)S(1)}, u32[]{:S(2)}, u32[]{:S(2)}) %collective-permute-start) | collective-permute-done | bytes 262176 | tf_op jit(solution)/shard_map/ppermute | solution.py:183
  22.5 3.7 %collective-permute-start.1 = (bf16[1024,128]{1,0:T(8,128)(2,1)S(1)}, bf16[1024,128]{1,0:T(8,128)(2,1)S(1)}, u32[]{:S(2)}, u32[]{:S(2)}) collective-permute-start(bf16[1024,128]{1,0:T(8,128)(2,1)S(1)} %collective-permute-done.refs_4_), channel_id=1, source_target_pairs={{0,1},{1,0},{2,3},{3,2},{4,5},{5,4},{6,7},{7,6},{8,9},{9,8},{10,11... | collective-permute-start | bytes 786440 | tf_op jit(solution)/shard_map/ppermute | solution.py:183
  26.3 0.0 copy-start
  26.3 1.2 %copy-done = bf16[512,1024]{1,0:T(8,128)(2,1)S(1)} copy-done((bf16[512,1024]{1,0:T(8,128)(2,1)S(1)}, bf16[512,1024]{1,0:T(8,128)(2,1)}, u32[]{:S(2)}) %copy-start) | copy-done | bytes 1048600
  27.5 4.3 %own.1 = (f32[512,1024]{1,0:T(8,128)S(1)}, f32[512,128]{1,0:T(8,128)S(1)}) custom-call(s32[1]{0:T(128)} %bitcast.refs_0_, s32[2,128]{1,0:T(2,128)S(1)} %add_subtract_fusion.refs_1_, bf16[512,1024]{1,0:T(8,128)(2,1)S(1)} %copy-done, bf16[1024,128]{1,0:T(8,128)(2,1)S(1)} %constant_dynamic-update-slice_fusion.refs_3_), custom_call_target="tpu_custom_call" | custom-call | flops 671088640 | bytes 3145728 | tf_op jit(solution)/shard_map/own/pallas_call | solution.py:143
  31.8 0.0 copy-start.1
  31.8 1.3 %copy-done.1 = f32[512,1024]{1,0:T(8,128)} copy-done((f32[512,1024]{1,0:T(8,128)}, f32[512,1024]{1,0:T(8,128)S(1)}, u32[]{:S(2)}) %copy-start.1) | copy-done | bytes 2097176
  33.1 0.0 collective-permute-done.2.refs_3_
  33.1 10.6 %sides.1 = (f32[512,1024]{1,0:T(8,128)S(1)}, f32[512,128]{1,0:T(8,128)S(1)}) custom-call(s32[1]{0:T(128)} %bitcast.refs_0_, s32[2,128]{1,0:T(2,128)S(1)} %add_subtract_fusion.refs_1_, bf16[512,1024]{1,0:T(8,128)(2,1)S(1)} %copy-done, bf16[1024,128]{1,0:T(8,128)(2,1)S(1)} %collective-permute-done.2.refs_3_, ...), custom_call_target="tpu_custom_call" | custom-call | flops 1744830464 | bytes 3145728 | tf_op jit(solution)/shard_map/sides/pallas_call | solution.py:143
  43.7 0.0 collective-permute-done.1.refs_3_
  43.7 11.0 %middle.1 = (bf16[512,1024]{1,0:T(8,128)(2,1)}, f32[512,128]{1,0:T(8,128)S(1)}) custom-call(s32[1]{0:T(128)} %bitcast.refs_0_, s32[2,128]{1,0:T(2,128)S(1)} %add_subtract_fusion.refs_1_, bf16[512,1024]{1,0:T(8,128)(2,1)S(1)} %copy-done, bf16[1024,128]{1,0:T(8,128)(2,1)S(1)} %collective-permute-done.1.refs_3_, f32[512,1024]{1,0:T(8,128)S(1)} %get-tuple-element.10.refs_4_, ...), custom_call_target="tpu_custom_call" | custom-call | flops 1073741824 | bytes 3145728 | tf_op jit(solution)/shard_map/middle/pallas_call | solution.py:143
  54.8 0.7 %copy.7 = f32[8,512]{1,0:T(8,128)} copy(f32[8,512]{0,1:T(8,128)S(1)} %multiply_bitcast_fusion) | data formatting | bytes 32768
  (2 shorter events, 0.0 us)
Async XLA Ops:
  2.5 20.1 %collective-permute-start = (bf16[1024,128]{1,0:T(8,128)(2,1)S(1)}, bf16[1024,128]{1,0:T(8,128)(2,1)S(1)}, u32[]{:S(2)}, u32[]{:S(2)}) collective-permute-start(bf16[1024,128]{1,0:T(8,128)(2,1)S(1)} %constant_dynamic-update-slice_fusion.refs_3_), channel_id=1, source_target_pairs={{0,3},{1,2},{2,5},{3,4},{4,7},{5,6},{6,9},{7,8},{8,11},{9,10},{10,... | collective-permute-start | bytes 786440 | tf_op jit(solution)/shard_map/ppermute | solution.py:183
  6.1 27.0 %collective-permute-start.2 = (bf16[1024,128]{1,0:T(8,128)(2,1)S(1)}, bf16[1024,128]{1,0:T(8,128)(2,1)S(1)}, u32[]{:S(2)}, u32[]{:S(2)}) collective-permute-start(bf16[1024,128]{1,0:T(8,128)(2,1)S(1)} %constant_dynamic-update-slice_fusion.refs_3_), channel_id=1, source_target_pairs={{0,1},{1,4},{2,3},{3,6},{4,5},{5,8},{6,7},{7,10},{8,9},{9,12},{10,... | collective-permute-start | bytes 786440 | tf_op jit(solution)/shard_map/ppermute | solution.py:183
  22.5 21.2 %collective-permute-start.1 = (bf16[1024,128]{1,0:T(8,128)(2,1)S(1)}, bf16[1024,128]{1,0:T(8,128)(2,1)S(1)}, u32[]{:S(2)}, u32[]{:S(2)}) collective-permute-start(bf16[1024,128]{1,0:T(8,128)(2,1)S(1)} %collective-permute-done.refs_4_), channel_id=1, source_target_pairs={{0,1},{1,0},{2,3},{3,2},{4,5},{5,4},{6,7},{7,6},{8,9},{9,8},{10,11... | collective-permute-start | bytes 786440 | tf_op jit(solution)/shard_map/ppermute | solution.py:183
  26.3 1.2 %copy-start = (bf16[512,1024]{1,0:T(8,128)(2,1)S(1)}, bf16[512,1024]{1,0:T(8,128)(2,1)}, u32[]{:S(2)}) copy-start(bf16[512,1024]{1,0:T(8,128)(2,1)} %refs_2_.5) | copy-start | bytes 3145732
  31.8 1.3 %copy-start.1 = (f32[512,1024]{1,0:T(8,128)}, f32[512,1024]{1,0:T(8,128)S(1)}, u32[]{:S(2)}) copy-start(f32[512,1024]{1,0:T(8,128)S(1)} %get-tuple-element.8.refs_5_) | copy-start | bytes 6291460

commit v2 on v0

v2 whole, which is shorter than its diff:
```python
import functools
import math

import jax
import jax.numpy as jnp
from jax import lax
from jax.experimental import pallas as pl
from jax.experimental.pallas import tpu as pltpu
from jax.sharding import PartitionSpec as P

AXES = ("outer", "inner")
LANES = 128
SIZE = 128
FAR = 2.0**15
LEAST, MOST = 2.0**-60, 2.0**100
TILE = 128
SCALE = SIZE**-0.5 * math.log2(math.e)
VMEM_BYTES = 32 * 1024 * 1024


def _dot_t(a, b):
    return lax.dot_general(a, b, (((1,), (1,)), ((), ())), preferred_element_type=jnp.float32)


def _document_ends(me, lengths, rows):
    lane = lax.broadcasted_iota(jnp.int32, (1, LANES), 1)
    at = -me[0] * rows
    first = jnp.full((1, LANES), 0, jnp.int32)
    last = first
    for d in range(lengths.shape[0]):
        first = jnp.where(lane == d, at, first)
        at = at + lengths[d]
        last = jnp.where(lane == d, at, last)
    return first, last


def _inside(ends, rows, offset):
    at = lax.broadcasted_iota(jnp.int32, (rows, LANES), 0) + offset
    return (at >= ends[0]) & (at < ends[1])


def _scores(q_ref, doc_s, key_s, i, tile, here):
    rs = slice(i * TILE, (i + 1) * TILE)
    start, count, _ = tile
    docs = doc_s[rs, :]
    left = [jnp.concatenate([q_ref[rs, h * SIZE : (h + 1) * SIZE], docs], axis=1) for h in range(here)]
    return _dot_t(jnp.concatenate(left, axis=0), key_s[start : start + count, :])


def _weigh(score, val_s, tile, here):
    start, count, (at, upper) = tile
    expon = jnp.exp2(score * SCALE).reshape(here, TILE, count)
    tri = lax.broadcasted_iota(jnp.int32, (1, TILE, TILE), 1) - lax.broadcasted_iota(jnp.int32, (1, TILE, TILE), 2)
    parts = [expon[:, :, :at]] if at else []
    parts.append(jnp.where(tri < 0 if upper else tri >= 0, expon[:, :, at : at + TILE], 0.0))
    if at + TILE < count:
        parts.append(expon[:, :, at + TILE :])
    expon = jnp.concatenate(parts, axis=2).reshape(here * TILE, count)
    total = jnp.sum(expon, axis=1, keepdims=True)
    num = jnp.dot(expon.astype(jnp.bfloat16), val_s[start : start + count, :], preferred_element_type=jnp.float32)
    return num, total


def _wide(x, g, width):
    return x.at[:, pl.ds(pl.multiple_of(g * width, width), width)]


def _own(me, lengths, q, k, v, num, sum_out, doc_out, q_s, num_s, key_s, val_s, doc_s, sums, sem_q, sem_n, sem):
    groups, rows, width = q_s.shape
    here = width // SIZE

    def copy_q(g):
        return pltpu.make_async_copy(_wide(q, g, width), q_s.at[g], sem_q.at[g])

    def copy_n(g):
        return pltpu.make_async_copy(num_s.at[g], _wide(num, g, width), sem_n.at[g])

    copy_k = pltpu.make_async_copy(k, key_s.at[:, 0:SIZE], sem.at[0])
    copy_v = pltpu.make_async_copy(v, val_s, sem.at[1])
    copy_d = pltpu.make_async_copy(doc_s, doc_out, sem.at[2])
    copy_s = pltpu.make_async_copy(sums, sum_out, sem.at[3])
    for copy in [copy_k, copy_v] + [copy_q(g) for g in range(groups)]:
        copy.start()
    ends = _document_ends(me, lengths, rows)
    for n in range(3):
        theirs = _inside(ends, rows, (n - 3) * rows)
        doc_s[n * rows : (n + 1) * rows, :] = jnp.where(theirs, 0.0, 1.0).astype(jnp.bfloat16)
    mine = _inside(ends, rows, 0)
    doc_s[3 * rows :, :] = jnp.where(mine, -FAR, 0.0).astype(jnp.bfloat16)
    copy_d.start()
    key_s[:, SIZE:] = jnp.where(mine, 0.0, 1.0).astype(jnp.bfloat16)
    sums[...] = jnp.zeros_like(sums)
    copy_k.wait()
    copy_v.wait()

    lane = lax.broadcasted_iota(jnp.int32, (TILE, LANES), 1)
    n = rows // TILE
    tiles = [(0, (i + 1) * TILE, (i * TILE, False)) for i in range(n)]
    docs = doc_s.at[3 * rows :]

    def group(g, carry):
        copy_q(g).wait()
        score = _scores(q_s.at[g], docs, key_s, 0, tiles[0], here)
        for i in range(n):
            following = _scores(q_s.at[g], docs, key_s, i + 1, tiles[i + 1], here) if i + 1 < n else None
            part, total = _weigh(score, val_s, tiles[i], here)
            rs = slice(i * TILE, (i + 1) * TILE)
            new = sums[rs, :]
            for h in range(here):
                hs = slice(h * TILE, (h + 1) * TILE)
                num_s[g, rs, h * SIZE : (h + 1) * SIZE] = part[hs]
                new = jnp.where(lane == g * here + h, total[hs], new)
            sums[rs, :] = new
            score = following
        copy_n(g).start()
        return carry

    lax.fori_loop(0, groups, group, 0)
    copy_s.start()
    for g in range(groups):
        copy_n(g).wait()
    copy_d.wait()
    copy_s.wait()


def _again(me, lengths, q_s, key_s, val_s, out_s, logs):
    groups, rows, width = q_s.shape
    ends = _document_ends(me, lengths, rows)
    depth, reach = 4 * rows, 3 * rows
    lane = lax.broadcasted_iota(jnp.int32, (TILE, LANES), 1)

    def tile(i, carry):
        rs = pl.ds(pl.multiple_of(i * TILE, TILE), TILE)
        begin = jnp.sum(jnp.where(_inside(ends, TILE, i * TILE), ends[0], 0), axis=1, keepdims=True)
        row = lax.broadcasted_iota(jnp.int32, (TILE, depth), 0) + i * TILE
        key = lax.broadcasted_iota(jnp.int32, (TILE, depth), 1) - reach
        allowed = (key <= row) & (row - key < reach) & (key >= begin)

        def group(g, carry):
            for h in range(width // SIZE):
                cols = slice(h * SIZE, (h + 1) * SIZE)
                score = _dot_t(q_s[g, rs, cols], key_s[...]) * SCALE
                score = jnp.where(allowed, score, -jnp.inf)
                top = jnp.max(score, axis=1, keepdims=True)
                expon = jnp.exp2(score - top)
                total = jnp.sum(expon, axis=1, keepdims=True)
                num = jnp.dot(expon.astype(jnp.bfloat16), val_s[...], preferred_element_type=jnp.float32)
                out_s[g, rs, cols] = (num / total).astype(out_s.dtype)
                mine = lane == g * (width // SIZE) + h
                logs[rs, :] = jnp.where(mine, top + jnp.log2(total), logs[rs, :])
            return carry

        return lax.fori_loop(0, groups, group, carry)

    lax.fori_loop(0, rows // TILE, tile, 0)


def _rest(me, lengths, q, chip, second, num, sum_in, docs, own_k, own_v, out, last,
          q_s, num_s, out_s, last_s, key_s, val_s, doc_s, sums, logs, sem_q, sem_n, sem_o, sem_k, sem_v, sem_d):
    groups, rows, width = q_s.shape
    here = width // SIZE
    even = lax.rem(me[0], 2) == 0
    places = [jnp.where(even, 2, 1), jnp.where(even, 1, 0), jnp.where(even, 0, 2)]
    at = [pl.ds(pl.multiple_of(place * rows, rows), rows) for place in places]
    blocks = (chip.at[0], chip.at[1], second)
    copy_k = [pltpu.make_async_copy(x.at[:, 0:SIZE], key_s.at[w], sem_k.at[n]) for n, (x, w) in enumerate(zip(blocks, at))]
    copy_v = [pltpu.make_async_copy(x.at[:, SIZE:], val_s.at[w], sem_v.at[n]) for n, (x, w) in enumerate(zip(blocks, at))]
    copy_d = [pltpu.make_async_copy(docs, doc_s, sem_d.at[0]), pltpu.make_async_copy(sum_in, sums, sem_d.at[1])]

    def copy_q(g):
        return pltpu.make_async_copy(_wide(q, g, width), q_s.at[g], sem_q.at[g])

    def copy_n(g):
        return pltpu.make_async_copy(_wide(num, g, width), num_s.at[g], sem_n.at[g])

    def copy_o(g):
        return pltpu.make_async_copy(out_s.at[g], _wide(out, g, width), sem_o.at[g])

    for copy in copy_k + copy_d[:1] + [copy_q(0)] + copy_v + copy_d[1:] + [copy_n(0)]:
        copy.start()
    for g in range(1, groups):
        copy_q(g).start()
        copy_n(g).start()
    for copy in copy_k + copy_d + copy_v:
        copy.wait()

    lane = lax.broadcasted_iota(jnp.int32, (TILE, LANES), 1)
    n = rows // TILE
    tiles = [(i * TILE, 3 * rows - i * TILE, (0, True)) for i in range(n)]

    def scores(g, i):
        start, count, _ = tiles[i]
        rs, keys = slice(i * TILE, (i + 1) * TILE), slice(start, start + count)
        mine = doc_s[3 * rows + i * TILE : 3 * rows + (i + 1) * TILE, :]
        left = [jnp.concatenate([q_s[g, rs, h * SIZE : (h + 1) * SIZE], mine], axis=1) for h in range(here)]
        right = jnp.concatenate([key_s[keys, :], doc_s[keys, :]], axis=1)
        return _dot_t(jnp.concatenate(left, axis=0), right)

    def group(g, carry):
        copy_q(g).wait()
        score = scores(g, 0)
        copy_n(g).wait()
        for i in range(n):
            following = scores(g, i + 1) if i + 1 < n else None
            part, total = _weigh(score, val_s, tiles[i], here)
            rs = slice(i * TILE, (i + 1) * TILE)
            new = sums[rs, :]
            for h in range(here):
                hs, cols = slice(h * TILE, (h + 1) * TILE), slice(h * SIZE, (h + 1) * SIZE)
                mine = lane == g * here + h
                whole = total[hs] + jnp.sum(jnp.where(mine, new, 0.0), axis=1, keepdims=True)
                out_s[g, rs, cols] = ((part[hs] + num_s[g, rs, cols]) * (1.0 / whole)).astype(out_s.dtype)
                new = jnp.where(mine, whole, new)
            sums[rs, :] = new
            score = following
        copy_o(g).start()
        return carry

    lax.fori_loop(0, groups, group, 0)

    heads = last.shape[0]
    copy_l = pltpu.make_async_copy(last_s, last, sem_d.at[0])
    total = sums[...]
    last_s[...] = jnp.transpose(jnp.log(total))[0:heads, :]
    copy_l.start()
    fine = (total >= LEAST) & (total <= MOST)
    used = lax.broadcasted_iota(jnp.int32, total.shape, 1) < heads
    wrong = jnp.max(jnp.where(used & jnp.logical_not(fine), 1.0, 0.0))
    for g in range(groups):
        copy_o(g).wait()
    copy_l.wait()

    @pl.when(wrong > 0.0)
    def _():
        own = pl.ds(3 * rows, rows)
        copies = [
            pltpu.make_async_copy(own_k, key_s.at[own], sem_k.at[0]),
            pltpu.make_async_copy(own_v, val_s.at[own], sem_v.at[0]),
        ]
        for copy in copies:
            copy.start()
        for copy in copies:
            copy.wait()
        _again(me, lengths, q_s, key_s, val_s, out_s, logs)
        last_s[...] = jnp.transpose(logs[...])[0:heads, :] * math.log(2.0)
        copy_l.start()
        for g in range(groups):
            copy_o(g).start()
        for g in range(groups):
            copy_o(g).wait()
        copy_l.wait()


SCALARS = pl.BlockSpec(memory_space=pltpu.SMEM)
ANYWHERE = pl.BlockSpec(memory_space=pl.ANY)
HBM = pl.BlockSpec(memory_space=pltpu.HBM)


def _join(k, v, both, sem):
    copies = [pltpu.make_async_copy(x, both.at[:, n * SIZE : (n + 1) * SIZE], sem.at[n]) for n, x in enumerate((k, v))]
    for copy in copies:
        copy.start()
    for copy in copies:
        copy.wait()


def _join_call(keys, values):
    rows, size = keys.shape
    return pl.pallas_call(
        _join,
        in_specs=[HBM, HBM],
        out_specs=ANYWHERE,
        out_shape=jax.ShapeDtypeStruct((rows, 2 * size), keys.dtype),
        scratch_shapes=[pltpu.SemaphoreType.DMA((2,))],
        compiler_params=pltpu.CompilerParams(vmem_limit_bytes=1024 * 1024),
        cost_estimate=pl.CostEstimate(flops=0, bytes_accessed=8 * rows * size, transcendentals=0),
        name="join",
    )(keys, values)


def _own_call(me, lengths, queries, keys, values, here):
    rows, width = queries.shape
    heads = width // SIZE
    groups = heads // here
    pairs = heads * rows * (rows + TILE) // 2
    return pl.pallas_call(
        _own,
        in_specs=[SCALARS, SCALARS, HBM, HBM, HBM],
        out_specs=[ANYWHERE] * 3,
        out_shape=[
            jax.ShapeDtypeStruct((rows, width), jnp.float32),
            jax.ShapeDtypeStruct((rows, LANES), jnp.float32),
            jax.ShapeDtypeStruct((4 * rows, LANES), jnp.bfloat16),
        ],
        scratch_shapes=[
            pltpu.VMEM((groups, rows, here * SIZE), jnp.bfloat16),
            pltpu.VMEM((groups, rows, here * SIZE), jnp.float32),
            pltpu.VMEM((rows, SIZE + LANES), jnp.bfloat16),
            pltpu.VMEM((rows, SIZE), jnp.bfloat16),
            pltpu.VMEM((4 * rows, LANES), jnp.bfloat16),
            pltpu.VMEM((rows, LANES), jnp.float32),
            pltpu.SemaphoreType.DMA((groups,)),
            pltpu.SemaphoreType.DMA((groups,)),
            pltpu.SemaphoreType.DMA((4,)),
        ],
        compiler_params=pltpu.CompilerParams(vmem_limit_bytes=VMEM_BYTES),
        cost_estimate=pl.CostEstimate(flops=4 * pairs * SIZE, bytes_accessed=6 * rows * width, transcendentals=pairs),
        name="own",
    )(me, lengths, queries, keys, values)


def _rest_call(me, lengths, queries, blocks, state, keys, values, here):
    rows, width = queries.shape
    heads = width // SIZE
    groups = heads // here
    pairs = heads * rows * (5 * rows + TILE) // 2
    return pl.pallas_call(
        _rest,
        in_specs=[SCALARS, SCALARS, HBM] + [ANYWHERE] * 5 + [HBM] * 2,
        out_specs=[HBM, HBM],
        out_shape=[
            jax.ShapeDtypeStruct((rows, width), queries.dtype),
            jax.ShapeDtypeStruct((heads, rows), jnp.float32),
        ],
        scratch_shapes=[
            pltpu.VMEM((groups, rows, here * SIZE), jnp.bfloat16),
            pltpu.VMEM((groups, rows, here * SIZE), jnp.float32),
            pltpu.VMEM((groups, rows, here * SIZE), jnp.bfloat16),
            pltpu.VMEM((heads, rows), jnp.float32),
            pltpu.VMEM((4 * rows, SIZE), jnp.bfloat16),
            pltpu.VMEM((4 * rows, SIZE), jnp.bfloat16),
            pltpu.VMEM((4 * rows, LANES), jnp.bfloat16),
            pltpu.VMEM((rows, LANES), jnp.float32),
            pltpu.VMEM((rows, LANES), jnp.float32),
            pltpu.SemaphoreType.DMA((groups,)),
            pltpu.SemaphoreType.DMA((groups,)),
            pltpu.SemaphoreType.DMA((groups,)),
            pltpu.SemaphoreType.DMA((3,)),
            pltpu.SemaphoreType.DMA((3,)),
            pltpu.SemaphoreType.DMA((2,)),
        ],
        compiler_params=pltpu.CompilerParams(vmem_limit_bytes=VMEM_BYTES),
        cost_estimate=pl.CostEstimate(flops=4 * pairs * SIZE, bytes_accessed=8 * rows * width, transcendentals=pairs),
        name="rest",
    )(me, lengths, queries, *blocks, *state, keys, values)


def shards(queries, keys, values, doc_lengths):
    count = lax.axis_size("outer") * lax.axis_size("inner")
    me = (lax.axis_index("outer") * lax.axis_size("inner") + lax.axis_index("inner")).astype(jnp.int32).reshape(1)

    def send(block, step_of):
        return lax.ppermute(
            block, AXES, [(i, i + step_of(i)) for i in range(count) if i + step_of(i) < count]
        )

    both = _join_call(keys, values)
    first = send(both, lambda i: 1 if i % 2 else 3)
    second = send(both, lambda i: 3 if i % 2 else 1)
    state = _own_call(me, doc_lengths, queries, keys, values, 2)
    first, state = lax.optimization_barrier((first, state))
    chip = lax.all_gather(first, AXES, axis_index_groups=[[i, i + 1] for i in range(0, count, 2)])
    blocks = (chip, second)
    return tuple(_rest_call(me, doc_lengths, queries, blocks, state, keys, values, 2))


def solution(mesh):
    placed = (P(AXES, None), P(AXES, None), P(AXES, None), P())
    return jax.shard_map(
        shards,
        mesh=mesh,
        in_specs=placed,
        out_specs=(P(AXES, None), P(None, AXES)),
        check_vma=False,
    )
```

time: 112 us -> 60.5 us (0.54)
  the two profiles are of different devices: /device:TPU:72 before, /device:TPU:8 now
where the time goes in v2:
time: 60.5 us; the launch traced here: 59.7 us
  Pallas kernels  38 us (63%)
  starting transfers between devices  6.23 us (10%)
  waiting for transfers between devices  5.71 us (9%)
  local copies, waits for them, and re-layouts  5.49 us (9%)
  blocking collectives  3.57 us (6%)
  between operations  0.69 us (1%)
    pallas_call x1, Pallas kernels, _rest_call(): pl.pallas_call(_rest, in_specs=[SCALARS, SCALARS, HBM] + [ANYWHERE] * 5 +...  33.6 us
    ppermute x2, starting transfers between devices, send(): lax.ppermute(block, AXES, [(i, i + step_of(i)) for i in range(count) if i...  6.23 us
    ppermute x2, waiting for transfers between devices, send(): lax.ppermute(block, AXES, [(i, i + step_of(i)) for i in range(count) if i...  5.71 us
    unnamed x12, local copies, waits for them, and re-layouts  5.49 us
    pallas_call x1, Pallas kernels, _own_call(): pl.pallas_call(_own, in_specs=[SCALARS, SCALARS, HBM, HBM, HBM], out_spec...  4.41 us
    all_gather x1, blocking collectives, shards(): lax.all_gather(first, AXES, axis_index_groups=[[i, i + 1] for i in range(...  3.57 us
  transfers between devices with their start and end apart: 2, of which 1 were waited for; matrix products, arithmetic and copies ran while one was open for 0% of the time, Pallas kernels for 7%

profile of v2, /device:TPU:8, one launch (start us, length us, event | category | flops | bytes accessed | tf_op | source)
XLA Modules:
  0.0 59.7 jit_solution(16873940508090451769)
XLA Ops:
  0.6 0.0 copy-start
  0.6 0.9 %copy-done = bf16[512,128]{1,0:T(8,128)(2,1)S(1)} copy-done((bf16[512,128]{1,0:T(8,128)(2,1)S(1)}, bf16[512,128]{1,0:T(8,128)(2,1)}, u32[]{:S(2)}) %copy-start) | copy-done | bytes 131096
  1.5 0.0 copy-start.2
  1.5 0.9 %copy-done.2 = bf16[512,128]{1,0:T(8,128)(2,1)S(1)} copy-done((bf16[512,128]{1,0:T(8,128)(2,1)S(1)}, bf16[512,128]{1,0:T(8,128)(2,1)}, u32[]{:S(2)}) %copy-start.2) | copy-done | bytes 131096
  2.4 0.1 join.1
  2.5 3.6 %collective-permute-start = (bf16[512,256]{1,0:T(8,128)(2,1)S(1)}, bf16[512,256]{1,0:T(8,128)(2,1)S(1)}, u32[]{:S(2)}, u32[]{:S(2)}) collective-permute-start(bf16[512,256]{1,0:T(8,128)(2,1)S(1)} %join.1), channel_id=1, source_target_pairs={{0,3},{1,2},{2,5},{3,4},{4,7},{5,6},{6,9},{7,8},{8,11},{9,10},{10,... | collective-permute-start | bytes 786440 | tf_op jit(solution)/shard_map/ppermute | solution.py:353
  6.2 2.6 %collective-permute-start.1 = (bf16[512,256]{1,0:T(8,128)(2,1)S(1)}, bf16[512,256]{1,0:T(8,128)(2,1)S(1)}, u32[]{:S(2)}, u32[]{:S(2)}) collective-permute-start(bf16[512,256]{1,0:T(8,128)(2,1)S(1)} %join.1), channel_id=1, source_target_pairs={{0,1},{1,4},{2,3},{3,6},{4,5},{5,8},{6,7},{7,10},{8,9},{9,12},{10,... | collective-permute-start | bytes 786440 | tf_op jit(solution)/shard_map/ppermute | solution.py:353
  8.8 0.0 copy-start.1
  8.8 0.9 %copy-done.1 = bf16[512,128]{1,0:T(8,128)(2,1)S(1)} copy-done((bf16[512,128]{1,0:T(8,128)(2,1)S(1)}, bf16[512,128]{1,0:T(8,128)(2,1)}, u32[]{:S(2)}) %copy-start.1) | copy-done | bytes 131096
  9.7 0.0 copy-start.3
  9.7 0.9 %copy-done.3 = bf16[512,128]{1,0:T(8,128)(2,1)S(1)} copy-done((bf16[512,128]{1,0:T(8,128)(2,1)S(1)}, bf16[512,128]{1,0:T(8,128)(2,1)}, u32[]{:S(2)}) %copy-start.3) | copy-done | bytes 131096
  10.6 0.0 copy-start.4
  10.6 1.2 %copy-done.4 = bf16[512,1024]{1,0:T(8,128)(2,1)S(1)} copy-done((bf16[512,1024]{1,0:T(8,128)(2,1)S(1)}, bf16[512,1024]{1,0:T(8,128)(2,1)}, u32[]{:S(2)}) %copy-start.4) | copy-done | bytes 1048600
  11.8 0.0 copy-start.5
  11.8 0.7 %copy-done.5 = s32[64]{0:T(128)S(1)} copy-done((s32[64]{0:T(128)S(1)}, s32[64]{0:T(128)}, u32[]{:S(2)}) %copy-start.5) | copy-done | bytes 280
  12.5 4.4 %own.1 = (f32[512,1024]{1,0:T(8,128)S(1)}, f32[512,128]{1,0:T(8,128)S(1)}, bf16[2048,128]{1,0:T(8,128)(2,1)S(1)}) custom-call(s32[1]{0:T(128)} %bitcast.me, s32[64]{0:T(128)S(1)} %copy-done.5, bf16[512,1024]{1,0:T(8,128)(2,1)S(1)} %copy-done.4, bf16[512,128]{1,0:T(8,128)(2,1)S(1)} %copy-done.1, bf16[512,128]{1,0:T(8,128)(2,1)S(1)} %copy-done.3), custom_call_target="tpu_custom_call" | custom-call | flops 671088640 | bytes 3145728 | tf_op jit(solution)/shard_map/own/pallas_call | solution.py:286
  16.9 5.7 %collective-permute-done = bf16[512,256]{1,0:T(8,128)(2,1)S(1)} collective-permute-done((bf16[512,256]{1,0:T(8,128)(2,1)S(1)}, bf16[512,256]{1,0:T(8,128)(2,1)S(1)}, u32[]{:S(2)}, u32[]{:S(2)}) %collective-permute-start) | collective-permute-done | bytes 262176 | tf_op jit(solution)/shard_map/ppermute | solution.py:353
  22.6 3.6 %all-gather = bf16[1024,256]{1,0:T(8,128)(2,1)S(1)} all-gather(bf16[512,256]{1,0:T(8,128)(2,1)S(1)} %collective-permute-done), channel_id=2, replica_groups={{0,1},{2,3},{4,5},{6,7},{8,9},{10,11},{12,13},{14,15},{16,17},{18,19},{..., dimensions={0}, use_global_device_ids=true | all-gather | bytes 786432 | tf_op jit(solution)/shard_map/all_gather | solution.py:362
  26.2 0.0 collective-permute-done.1.second
  26.2 33.6 %rest.1 = (bf16[512,1024]{1,0:T(8,128)(2,1)}, f32[8,512]{1,0:T(8,128)}) custom-call(s32[1]{0:T(128)} %bitcast.me, s32[64]{0:T(128)S(1)} %copy-done.5, bf16[512,1024]{1,0:T(8,128)(2,1)S(1)} %copy-done.4, bf16[2,512,256]{2,1,0:T(8,128)(2,1)S(1)} %bitcast.2, bf16[512,256]{1,0:T(8,128)(2,1)S(1)} %collective-permute-done.1.second, ...), custom_call_target="tpu_custom_call" | custom-call | flops 2818572288 | bytes 4194304 | tf_op jit(solution)/shard_map/rest/pallas_call | solution.py:317
Async XLA Ops:
  0.6 0.9 %copy-start = (bf16[512,128]{1,0:T(8,128)(2,1)S(1)}, bf16[512,128]{1,0:T(8,128)(2,1)}, u32[]{:S(2)}) copy-start(bf16[512,128]{1,0:T(8,128)(2,1)} %own_k.1) | copy-start | bytes 393220
  1.5 0.9 %copy-start.2 = (bf16[512,128]{1,0:T(8,128)(2,1)S(1)}, bf16[512,128]{1,0:T(8,128)(2,1)}, u32[]{:S(2)}) copy-start(bf16[512,128]{1,0:T(8,128)(2,1)} %own_v.1) | copy-start | bytes 393220
  2.5 20.1 %collective-permute-start = (bf16[512,256]{1,0:T(8,128)(2,1)S(1)}, bf16[512,256]{1,0:T(8,128)(2,1)S(1)}, u32[]{:S(2)}, u32[]{:S(2)}) collective-permute-start(bf16[512,256]{1,0:T(8,128)(2,1)S(1)} %join.1), channel_id=1, source_target_pairs={{0,3},{1,2},{2,5},{3,4},{4,7},{5,6},{6,9},{7,8},{8,11},{9,10},{10,... | collective-permute-start | bytes 786440 | tf_op jit(solution)/shard_map/ppermute | solution.py:353
  6.2 20.0 %collective-permute-start.1 = (bf16[512,256]{1,0:T(8,128)(2,1)S(1)}, bf16[512,256]{1,0:T(8,128)(2,1)S(1)}, u32[]{:S(2)}, u32[]{:S(2)}) collective-permute-start(bf16[512,256]{1,0:T(8,128)(2,1)S(1)} %join.1), channel_id=1, source_target_pairs={{0,1},{1,4},{2,3},{3,6},{4,5},{5,8},{6,7},{7,10},{8,9},{9,12},{10,... | collective-permute-start | bytes 786440 | tf_op jit(solution)/shard_map/ppermute | solution.py:353
  8.8 0.9 %copy-start.1 = (bf16[512,128]{1,0:T(8,128)(2,1)S(1)}, bf16[512,128]{1,0:T(8,128)(2,1)}, u32[]{:S(2)}) copy-start(bf16[512,128]{1,0:T(8,128)(2,1)} %own_k.1) | copy-start | bytes 393220
  9.7 0.9 %copy-start.3 = (bf16[512,128]{1,0:T(8,128)(2,1)S(1)}, bf16[512,128]{1,0:T(8,128)(2,1)}, u32[]{:S(2)}) copy-start(bf16[512,128]{1,0:T(8,128)(2,1)} %own_v.1) | copy-start | bytes 393220
  10.6 1.2 %copy-start.4 = (bf16[512,1024]{1,0:T(8,128)(2,1)S(1)}, bf16[512,1024]{1,0:T(8,128)(2,1)}, u32[]{:S(2)}) copy-start(bf16[512,1024]{1,0:T(8,128)(2,1)} %q.3) | copy-start | bytes 3145732
  11.8 0.7 %copy-start.5 = (s32[64]{0:T(128)S(1)}, s32[64]{0:T(128)}, u32[]{:S(2)}) copy-start(s32[64]{0:T(128)} %lengths.3) | copy-start | bytes 772

commit v3 on v2

v3 whole, which is shorter than its diff:
```python
import functools
import math

import jax
import jax.numpy as jnp
from jax import lax
from jax.experimental import pallas as pl
from jax.experimental.pallas import tpu as pltpu
from jax.sharding import PartitionSpec as P

AXES = ("outer", "inner")
LANES = 128
SIZE = 128
FAR = 2.0**15
LEAST, MOST = 2.0**-60, 2.0**100
TILE = 128
SCALE = SIZE**-0.5 * math.log2(math.e)
VMEM_BYTES = 32 * 1024 * 1024


def _dot_t(a, b):
    return lax.dot_general(a, b, (((1,), (1,)), ((), ())), preferred_element_type=jnp.float32)


def _document_ends(me, lengths, rows):
    lane = lax.broadcasted_iota(jnp.int32, (1, LANES), 1)
    at = -me[0] * rows
    first = jnp.full((1, LANES), 0, jnp.int32)
    last = first
    for d in range(lengths.shape[0]):
        first = jnp.where(lane == d, at, first)
        at = at + lengths[d]
        last = jnp.where(lane == d, at, last)
    return first, last


def _inside(ends, rows, offset):
    at = lax.broadcasted_iota(jnp.int32, (rows, LANES), 0) + offset
    return (at >= ends[0]) & (at < ends[1])


def _scores(q_ref, doc_s, key_s, i, tile, here):
    rs = slice(i * TILE, (i + 1) * TILE)
    start, count, _ = tile
    docs = doc_s[rs, :]
    left = [jnp.concatenate([q_ref[rs, h * SIZE : (h + 1) * SIZE], docs], axis=1) for h in range(here)]
    return _dot_t(jnp.concatenate(left, axis=0), key_s[start : start + count, :])


def _weigh(score, val_s, tile, here):
    start, count, (at, upper) = tile
    expon = jnp.exp2(score * SCALE).reshape(here, TILE, count)
    tri = lax.broadcasted_iota(jnp.int32, (1, TILE, TILE), 1) - lax.broadcasted_iota(jnp.int32, (1, TILE, TILE), 2)
    parts = [expon[:, :, :at]] if at else []
    parts.append(jnp.where(tri < 0 if upper else tri >= 0, expon[:, :, at : at + TILE], 0.0))
    if at + TILE < count:
        parts.append(expon[:, :, at + TILE :])
    expon = jnp.concatenate(parts, axis=2).reshape(here * TILE, count)
    num = jnp.dot(expon.astype(jnp.bfloat16), val_s[start : start + count, :], preferred_element_type=jnp.float32)
    return num[:, 0:SIZE], num[:, SIZE:]


def _own(me, lengths, q, both, num, sums, docs, key_s, val_s):
    rows, width = q.shape
    here = width // SIZE
    n = rows // TILE
    ends = _document_ends(me, lengths, rows)
    for back in range(3):
        theirs = _inside(ends, rows, (back - 3) * rows)
        docs[back * rows : (back + 1) * rows, :] = jnp.where(theirs, 0.0, 1.0).astype(jnp.bfloat16)
    mine = _inside(ends, rows, 0)
    docs[3 * rows :, :] = jnp.where(mine, -FAR, 0.0).astype(jnp.bfloat16)
    key_s[:, 0:SIZE] = both[:, 0:SIZE]
    key_s[:, SIZE:] = jnp.where(mine, 0.0, 1.0).astype(jnp.bfloat16)
    val_s[:, 0:SIZE] = both[:, SIZE:]
    val_s[:, SIZE:] = jnp.ones((rows, LANES), jnp.bfloat16)

    lane = lax.broadcasted_iota(jnp.int32, (TILE, LANES), 1)
    tiles = [(0, (i + 1) * TILE, (i * TILE, False)) for i in range(n)]
    my_docs = docs.at[3 * rows :]
    score = _scores(q, my_docs, key_s, 0, tiles[0], here)
    for i in range(n):
        rs = slice(i * TILE, (i + 1) * TILE)
        following = _scores(q, my_docs, key_s, i + 1, tiles[i + 1], here) if i + 1 < n else None
        part, total = _weigh(score, val_s, tiles[i], here)
        new = jnp.zeros((TILE, LANES), jnp.float32)
        for h in range(here):
            hs = slice(h * TILE, (h + 1) * TILE)
            num[rs, h * SIZE : (h + 1) * SIZE] = part[hs]
            new = jnp.where(lane == h, total[hs], new)
        sums[rs, :] = new
        score = following


def _again(me, lengths, q, key_s, val_s, out_s, logs):
    rows, width = q.shape
    ends = _document_ends(me, lengths, rows)
    depth, reach = 4 * rows, 3 * rows
    lane = lax.broadcasted_iota(jnp.int32, (TILE, LANES), 1)

    def tile(i, carry):
        rs = pl.ds(pl.multiple_of(i * TILE, TILE), TILE)
        begin = jnp.sum(jnp.where(_inside(ends, TILE, i * TILE), ends[0], 0), axis=1, keepdims=True)
        row = lax.broadcasted_iota(jnp.int32, (TILE, depth), 0) + i * TILE
        key = lax.broadcasted_iota(jnp.int32, (TILE, depth), 1) - reach
        allowed = (key <= row) & (row - key < reach) & (key >= begin)

        def head(h, carry):
            cols = pl.ds(pl.multiple_of(h * SIZE, SIZE), SIZE)
            score = _dot_t(q[rs, cols], key_s[...]) * SCALE
            score = jnp.where(allowed, score, -jnp.inf)
            top = jnp.max(score, axis=1, keepdims=True)
            expon = jnp.exp2(score - top)
            total = jnp.sum(expon, axis=1, keepdims=True)
            num = jnp.dot(expon.astype(jnp.bfloat16), val_s[:, 0:SIZE], preferred_element_type=jnp.float32)
            out_s[rs, cols] = (num / total).astype(out_s.dtype)
            logs[rs, :] = jnp.where(lane == h, top + jnp.log2(total), logs[rs, :])
            return carry

        return lax.fori_loop(0, width // SIZE, head, carry)

    lax.fori_loop(0, rows // TILE, tile, 0)


def _rest(me, lengths, q, chip, second, num, sums, docs, both, out, last,
          out_s, last_s, key_s, val_s, logs, sem_o, sem_k, sem_v, sem_l):
    rows, width = q.shape
    here = width // SIZE
    n = rows // TILE
    even = lax.rem(me[0], 2) == 0
    places = [jnp.where(even, 2, 1), jnp.where(even, 1, 0), jnp.where(even, 0, 2)]
    at = [pl.ds(pl.multiple_of(place * rows, rows), rows) for place in places]
    blocks = (chip.at[0], chip.at[1], second)
    copy_k = [pltpu.make_async_copy(x.at[:, 0:SIZE], key_s.at[w], sem_k.at[j]) for j, (x, w) in enumerate(zip(blocks, at))]
    copy_v = [
        pltpu.make_async_copy(x.at[:, SIZE:], val_s.at[w, 0:SIZE], sem_v.at[j]) for j, (x, w) in enumerate(zip(blocks, at))
    ]
    spans = [slice(i * TILE, (i + 1) * TILE) for i in range(n)]
    copy_o = [pltpu.make_async_copy(out_s.at[rs], out.at[rs], sem_o.at[i]) for i, rs in enumerate(spans)]
    copy_l = pltpu.make_async_copy(last_s, last, sem_l)
    for copy in copy_k + copy_v:
        copy.start()
    val_s[0 : 3 * rows, SIZE:] = jnp.ones((3 * rows, LANES), jnp.bfloat16)
    for copy in copy_k + copy_v:
        copy.wait()

    lane = lax.broadcasted_iota(jnp.int32, (TILE, LANES), 1)
    tiles = [(i * TILE, 3 * rows - i * TILE, (0, True)) for i in range(n)]

    def scores(i):
        start, count, _ = tiles[i]
        rs, keys = spans[i], slice(start, start + count)
        mine = docs[3 * rows + i * TILE : 3 * rows + (i + 1) * TILE, :]
        left = [jnp.concatenate([q[rs, h * SIZE : (h + 1) * SIZE], mine], axis=1) for h in range(here)]
        right = jnp.concatenate([key_s[keys, :], docs[keys, :]], axis=1)
        return _dot_t(jnp.concatenate(left, axis=0), right)

    score = scores(0)
    for i, rs in enumerate(spans):
        following = scores(i + 1) if i + 1 < n else None
        part, total = _weigh(score, val_s, tiles[i], here)
        before = sums[rs, :]
        log = jnp.zeros((TILE, LANES), jnp.float32)
        for h in range(here):
            hs, cols = slice(h * TILE, (h + 1) * TILE), slice(h * SIZE, (h + 1) * SIZE)
            whole = total[hs] + jnp.broadcast_to(before[:, h : h + 1], (TILE, LANES))
            out_s[rs, cols] = ((part[hs] + num[rs, cols]) * (1.0 / whole)).astype(out_s.dtype)
            log = jnp.where(lane == h, whole, log)
        logs[rs, :] = log
        copy_o[i].start()
        score = following

    heads = last.shape[0]
    total = logs[...]
    last_s[...] = jnp.transpose(jnp.log(total))[0:heads, :]
    copy_l.start()
    fine = (total >= LEAST) & (total <= MOST)
    used = lax.broadcasted_iota(jnp.int32, total.shape, 1) < heads
    wrong = jnp.max(jnp.where(used & jnp.logical_not(fine), 1.0, 0.0))
    for copy in copy_o + [copy_l]:
        copy.wait()

    @pl.when(wrong > 0.0)
    def _():
        own = pl.ds(3 * rows, rows)
        copies = [
            pltpu.make_async_copy(both.at[:, 0:SIZE], key_s.at[own], sem_k.at[0]),
            pltpu.make_async_copy(both.at[:, SIZE:], val_s.at[own, 0:SIZE], sem_v.at[0]),
        ]
        for copy in copies:
            copy.start()
        for copy in copies:
            copy.wait()
        _again(me, lengths, q, key_s, val_s, out_s, logs)
        last_s[...] = jnp.transpose(logs[...])[0:heads, :] * math.log(2.0)
        for copy in copy_o + [copy_l]:
            copy.start()
        for copy in copy_o + [copy_l]:
            copy.wait()


SCALARS = pl.BlockSpec(memory_space=pltpu.SMEM)
ANYWHERE = pl.BlockSpec(memory_space=pl.ANY)
HBM = pl.BlockSpec(memory_space=pltpu.HBM)
VMEM = pl.BlockSpec(memory_space=pltpu.VMEM)


def _join(k, v, both, sem):
    copies = [pltpu.make_async_copy(x, both.at[:, n * SIZE : (n + 1) * SIZE], sem.at[n]) for n, x in enumerate((k, v))]
    for copy in copies:
        copy.start()
    for copy in copies:
        copy.wait()


def _join_call(keys, values):
    rows, size = keys.shape
    return pl.pallas_call(
        _join,
        in_specs=[HBM, HBM],
        out_specs=ANYWHERE,
        out_shape=jax.ShapeDtypeStruct((rows, 2 * size), keys.dtype),
        scratch_shapes=[pltpu.SemaphoreType.DMA((2,))],
        compiler_params=pltpu.CompilerParams(vmem_limit_bytes=1024 * 1024),
        cost_estimate=pl.CostEstimate(flops=0, bytes_accessed=8 * rows * size, transcendentals=0),
        name="join",
    )(keys, values)


def _own_call(me, lengths, queries, both):
    rows, width = queries.shape
    pairs = width // SIZE * rows * (rows + TILE) // 2
    return pl.pallas_call(
        _own,
        in_specs=[SCALARS, SCALARS, VMEM, VMEM],
        out_specs=[VMEM] * 3,
        out_shape=[
            jax.ShapeDtypeStruct((rows, width), jnp.float32),
            jax.ShapeDtypeStruct((rows, LANES), jnp.float32),
            jax.ShapeDtypeStruct((4 * rows, LANES), jnp.bfloat16),
        ],
        scratch_shapes=[
            pltpu.VMEM((rows, SIZE + LANES), jnp.bfloat16),
            pltpu.VMEM((rows, SIZE + LANES), jnp.bfloat16),
        ],
        compiler_params=pltpu.CompilerParams(vmem_limit_bytes=VMEM_BYTES),
        cost_estimate=pl.CostEstimate(flops=4 * pairs * SIZE, bytes_accessed=6 * rows * width, transcendentals=pairs),
        name="own",
    )(me, lengths, queries, both)


def _rest_call(me, lengths, queries, blocks, state, both):
    rows, width = queries.shape
    heads = width // SIZE
    pairs = heads * rows * (5 * rows + TILE) // 2
    return pl.pallas_call(
        _rest,
        in_specs=[SCALARS, SCALARS, VMEM, ANYWHERE, ANYWHERE, VMEM, VMEM, VMEM, ANYWHERE],
        out_specs=[HBM, HBM],
        out_shape=[
            jax.ShapeDtypeStruct((rows, width), queries.dtype),
            jax.ShapeDtypeStruct((heads, rows), jnp.float32),
        ],
        scratch_shapes=[
            pltpu.VMEM((rows, width), jnp.bfloat16),
            pltpu.VMEM((heads, rows), jnp.float32),
            pltpu.VMEM((4 * rows, SIZE), jnp.bfloat16),
            pltpu.VMEM((4 * rows, SIZE + LANES), jnp.bfloat16),
            pltpu.VMEM((rows, LANES), jnp.float32),
            pltpu.SemaphoreType.DMA((rows // TILE,)),
            pltpu.SemaphoreType.DMA((3,)),
            pltpu.SemaphoreType.DMA((3,)),
            pltpu.SemaphoreType.DMA,
        ],
        compiler_params=pltpu.CompilerParams(vmem_limit_bytes=VMEM_BYTES),
        cost_estimate=pl.CostEstimate(flops=4 * pairs * SIZE, bytes_accessed=8 * rows * width, transcendentals=pairs),
        name="rest",
    )(me, lengths, queries, *blocks, *state, both)


def shards(queries, keys, values, doc_lengths):
    count = lax.axis_size("outer") * lax.axis_size("inner")
    me = (lax.axis_index("outer") * lax.axis_size("inner") + lax.axis_index("inner")).astype(jnp.int32).reshape(1)

    def send(block, step_of):
        return lax.ppermute(
            block, AXES, [(i, i + step_of(i)) for i in range(count) if i + step_of(i) < count]
        )

    both = _join_call(*(pltpu.with_memory_space_constraint(x, pltpu.HBM) for x in (keys, values)))
    first = send(both, lambda i: 1 if i % 2 else 3)
    second = send(both, lambda i: 3 if i % 2 else 1)
    state = _own_call(me, doc_lengths, queries, both)
    first, state = lax.optimization_barrier((first, state))
    chip = lax.all_gather(first, AXES, axis_index_groups=[[i, i + 1] for i in range(0, count, 2)])
    blocks = (chip, second)
    return tuple(_rest_call(me, doc_lengths, queries, blocks, state, both))


def solution(mesh):
    placed = (P(AXES, None), P(AXES, None), P(AXES, None), P())
    return jax.shard_map(
        shards,
        mesh=mesh,
        in_specs=placed,
        out_specs=(P(AXES, None), P(None, AXES)),
        check_vma=False,
    )
```

time: 60.5 us -> 62 us (1.025)
  waiting for transfers between devices: 5.71 us -> 9.39 us
  local copies, waits for them, and re-layouts: 5.49 us -> 1.87 us
  Pallas kernels: 38 us -> 39.5 us
    ppermute x2, waiting for transfers between devices: 5.71 us -> 9.39 us  [send(): lax.ppermute(block, AXES, [(i, i + step_of(i)) for i in range(count) if i...]
    unnamed x12 -> x4, local copies, waits for them, and re-layouts: 5.49 us -> 1.87 us
    pallas_call x1, Pallas kernels: 0.07 us -> 0.99 us  [_join_call(): pl.pallas_call(_join, in_specs=[HBM, HBM], out_specs=ANYWHERE, out_shape=...]
  transfers between devices with their start and end apart: 2 -> 2, of which waited for: 1 -> 1; matrix products, arithmetic and copies ran while one was open for 0% -> 0% of each run, Pallas kernels for 7% -> 4%
where the time goes in v3:
time: 62 us; the launch traced here: 61.3 us
  Pallas kernels  39.5 us (64%)
  waiting for transfers between devices  9.39 us (15%)
  starting transfers between devices  6.23 us (10%)
  blocking collectives  3.57 us (6%)
  local copies, waits for them, and re-layouts  1.87 us (3%)
  between operations  0.68 us (1%)
    pallas_call x1, Pallas kernels, _rest_call(): pl.pallas_call(_rest, in_specs=[SCALARS, SCALARS, VMEM, ANYWHERE, ANYWHER...  36 us
    ppermute x2, waiting for transfers between devices, send(): lax.ppermute(block, AXES, [(i, i + step_of(i)) for i in range(count) if i...  9.39 us
    ppermute x2, starting transfers between devices, send(): lax.ppermute(block, AXES, [(i, i + step_of(i)) for i in range(count) if i...  6.23 us
    all_gather x1, blocking collectives, shards(): lax.all_gather(first, AXES, axis_index_groups=[[i, i + 1] for i in range(...  3.57 us
    pallas_call x1, Pallas kernels, _own_call(): pl.pallas_call(_own, in_specs=[SCALARS, SCALARS, VMEM, VMEM], out_specs=[...  2.55 us
    unnamed x4, local copies, waits for them, and re-layouts  1.87 us
  transfers between devices with their start and end apart: 2, of which 1 were waited for; matrix products, arithmetic and copies ran while one was open for 0% of the time, Pallas kernels for 4%

profile of v3, /device:TPU:8, one launch (start us, length us, event | category | flops | bytes accessed | tf_op | source)
XLA Modules:
  0.0 61.3 jit_solution(10706452432478967242)
XLA Ops:
  0.6 1.0 %join.1.both = bf16[512,256]{1,0:T(8,128)(2,1)S(1)} custom-call(bf16[512,128]{1,0:T(8,128)(2,1)} %k.1, bf16[512,128]{1,0:T(8,128)(2,1)} %v.1), custom_call_target="tpu_custom_call" | custom-call | bytes 524288 | tf_op jit(solution)/shard_map/join/pallas_call | solution.py:218
  1.6 3.6 %collective-permute-start = (bf16[512,256]{1,0:T(8,128)(2,1)S(1)}, bf16[512,256]{1,0:T(8,128)(2,1)S(1)}, u32[]{:S(2)}, u32[]{:S(2)}) collective-permute-start(bf16[512,256]{1,0:T(8,128)(2,1)S(1)} %join.1.both), channel_id=1, source_target_pairs={{0,3},{1,2},{2,5},{3,4},{4,7},{5,6},{6,9},{7,8},{8,11},{9,10},{10,... | collective-permute-start | bytes 786440 | tf_op jit(solution)/shard_map/ppermute | solution.py:286
  5.3 2.6 %collective-permute-start.1 = (bf16[512,256]{1,0:T(8,128)(2,1)S(1)}, bf16[512,256]{1,0:T(8,128)(2,1)S(1)}, u32[]{:S(2)}, u32[]{:S(2)}) collective-permute-start(bf16[512,256]{1,0:T(8,128)(2,1)S(1)} %join.1.both), channel_id=1, source_target_pairs={{0,1},{1,4},{2,3},{3,6},{4,5},{5,8},{6,7},{7,10},{8,9},{9,12},{10,... | collective-permute-start | bytes 786440 | tf_op jit(solution)/shard_map/ppermute | solution.py:286
  7.9 0.0 copy-start
  7.9 1.2 %copy-done = bf16[512,1024]{1,0:T(8,128)(2,1)S(1)} copy-done((bf16[512,1024]{1,0:T(8,128)(2,1)S(1)}, bf16[512,1024]{1,0:T(8,128)(2,1)}, u32[]{:S(2)}) %copy-start) | copy-done | bytes 1048600
  9.1 0.0 copy-start.1
  9.1 0.7 %copy-done.1 = s32[64]{0:T(128)S(1)} copy-done((s32[64]{0:T(128)S(1)}, s32[64]{0:T(128)}, u32[]{:S(2)}) %copy-start.1) | copy-done | bytes 280
  9.8 2.5 %own.1 = (f32[512,1024]{1,0:T(8,128)S(1)}, f32[512,128]{1,0:T(8,128)S(1)}, bf16[2048,128]{1,0:T(8,128)(2,1)S(1)}) custom-call(s32[1]{0:T(128)} %bitcast.me, s32[64]{0:T(128)S(1)} %copy-done.1, bf16[512,1024]{1,0:T(8,128)(2,1)S(1)} %copy-done, bf16[512,256]{1,0:T(8,128)(2,1)S(1)} %join.1.both), custom_call_target="tpu_custom_call" | custom-call | flops 671088640 | bytes 3145728 | tf_op jit(solution)/shard_map/own/pallas_call | solution.py:233
  12.3 9.4 %collective-permute-done = bf16[512,256]{1,0:T(8,128)(2,1)S(1)} collective-permute-done((bf16[512,256]{1,0:T(8,128)(2,1)S(1)}, bf16[512,256]{1,0:T(8,128)(2,1)S(1)}, u32[]{:S(2)}, u32[]{:S(2)}) %collective-permute-start) | collective-permute-done | bytes 262176 | tf_op jit(solution)/shard_map/ppermute | solution.py:286
  21.7 3.6 %all-gather = bf16[1024,256]{1,0:T(8,128)(2,1)S(1)} all-gather(bf16[512,256]{1,0:T(8,128)(2,1)S(1)} %collective-permute-done), channel_id=2, replica_groups={{0,1},{2,3},{4,5},{6,7},{8,9},{10,11},{12,13},{14,15},{16,17},{18,19},{..., dimensions={0}, use_global_device_ids=true | all-gather | bytes 786432 | tf_op jit(solution)/shard_map/all_gather | solution.py:295
  25.3 0.0 collective-permute-done.1.second
  25.3 36.0 %rest.1 = (bf16[512,1024]{1,0:T(8,128)(2,1)}, f32[8,512]{1,0:T(8,128)}) custom-call(s32[1]{0:T(128)} %bitcast.me, s32[64]{0:T(128)S(1)} %copy-done.1, bf16[512,1024]{1,0:T(8,128)(2,1)S(1)} %copy-done, bf16[2,512,256]{2,1,0:T(8,128)(2,1)S(1)} %bitcast.2, bf16[512,256]{1,0:T(8,128)(2,1)S(1)} %collective-permute-done.1.second, ...), custom_call_target="tpu_custom_call" | custom-call | flops 2818572288 | bytes 4194304 | tf_op jit(solution)/shard_map/rest/pallas_call | solution.py:256
Async XLA Ops:
  1.6 20.1 %collective-permute-start = (bf16[512,256]{1,0:T(8,128)(2,1)S(1)}, bf16[512,256]{1,0:T(8,128)(2,1)S(1)}, u32[]{:S(2)}, u32[]{:S(2)}) collective-permute-start(bf16[512,256]{1,0:T(8,128)(2,1)S(1)} %join.1.both), channel_id=1, source_target_pairs={{0,3},{1,2},{2,5},{3,4},{4,7},{5,6},{6,9},{7,8},{8,11},{9,10},{10,... | collective-permute-start | bytes 786440 | tf_op jit(solution)/shard_map/ppermute | solution.py:286
  5.3 20.0 %collective-permute-start.1 = (bf16[512,256]{1,0:T(8,128)(2,1)S(1)}, bf16[512,256]{1,0:T(8,128)(2,1)S(1)}, u32[]{:S(2)}, u32[]{:S(2)}) collective-permute-start(bf16[512,256]{1,0:T(8,128)(2,1)S(1)} %join.1.both), channel_id=1, source_target_pairs={{0,1},{1,4},{2,3},{3,6},{4,5},{5,8},{6,7},{7,10},{8,9},{9,12},{10,... | collective-permute-start | bytes 786440 | tf_op jit(solution)/shard_map/ppermute | solution.py:286
  7.9 1.2 %copy-start = (bf16[512,1024]{1,0:T(8,128)(2,1)S(1)}, bf16[512,1024]{1,0:T(8,128)(2,1)}, u32[]{:S(2)}) copy-start(bf16[512,1024]{1,0:T(8,128)(2,1)} %q.3) | copy-start | bytes 3145732
  9.1 0.7 %copy-start.1 = (s32[64]{0:T(128)S(1)}, s32[64]{0:T(128)}, u32[]{:S(2)}) copy-start(s32[64]{0:T(128)} %lengths.3) | copy-start | bytes 772

commit v4 on v3

--- a/solution.py
+++ b/solution.py
@@ -122,7 +122,7 @@
     lax.fori_loop(0, rows // TILE, tile, 0)
 
 
-def _rest(me, lengths, q, chip, second, num, sums, docs, both, out, last,
+def _rest(me, lengths, q, chip, second, late, num, sums, docs, both, out, last,
           out_s, last_s, key_s, val_s, logs, sem_o, sem_k, sem_v, sem_l):
     rows, width = q.shape
     here = width // SIZE
@@ -138,7 +138,19 @@
     spans = [slice(i * TILE, (i + 1) * TILE) for i in range(n)]
     copy_o = [pltpu.make_async_copy(out_s.at[rs], out.at[rs], sem_o.at[i]) for i, rs in enumerate(spans)]
     copy_l = pltpu.make_async_copy(last_s, last, sem_l)
-    for copy in copy_k + copy_v:
+    is_late = me[0] == me[1]
+
+    @pl.when(is_late)
+    def _():
+        pltpu.make_async_copy(late.at[:, 0:SIZE], key_s.at[at[2]], sem_k.at[2]).start()
+        pltpu.make_async_copy(late.at[:, SIZE:], val_s.at[at[2], 0:SIZE], sem_v.at[2]).start()
+
+    @pl.when(jnp.logical_not(is_late))
+    def _():
+        copy_k[2].start()
+        copy_v[2].start()
+
+    for copy in copy_k[:2] + copy_v[:2]:
         copy.start()
     val_s[0 : 3 * rows, SIZE:] = jnp.ones((3 * rows, LANES), jnp.bfloat16)
     for copy in copy_k + copy_v:
@@ -255,7 +267,7 @@
     pairs = heads * rows * (5 * rows + TILE) // 2
     return pl.pallas_call(
         _rest,
-        in_specs=[SCALARS, SCALARS, VMEM, ANYWHERE, ANYWHERE, VMEM, VMEM, VMEM, ANYWHERE],
+        in_specs=[SCALARS, SCALARS, VMEM, ANYWHERE, ANYWHERE, ANYWHERE, VMEM, VMEM, VMEM, ANYWHERE],
         out_specs=[HBM, HBM],
         out_shape=[
             jax.ShapeDtypeStruct((rows, width), queries.dtype),
@@ -280,20 +292,22 @@
 
 def shards(queries, keys, values, doc_lengths):
     count = lax.axis_size("outer") * lax.axis_size("inner")
-    me = (lax.axis_index("outer") * lax.axis_size("inner") + lax.axis_index("inner")).astype(jnp.int32).reshape(1)
-
-    def send(block, step_of):
-        return lax.ppermute(
-            block, AXES, [(i, i + step_of(i)) for i in range(count) if i + step_of(i) < count]
-        )
-
+    me = (lax.axis_index("outer") * lax.axis_size("inner") + lax.axis_index("inner")).astype(jnp.int32)
+    me = jnp.stack([me, jnp.int32(count // 2)])
+
+    def send(block, step_of, chosen=lambda i: True):
+        pairs = [(i, i + step_of(i)) for i in range(count) if i + step_of(i) < count and chosen(i)]
+        return lax.ppermute(block, AXES, pairs)
+
+    first = [send(x, lambda i: 1 if i % 2 else 3) for x in (keys, values)]
     both = _join_call(*(pltpu.with_memory_space_constraint(x, pltpu.HBM) for x in (keys, values)))
-    first = send(both, lambda i: 1 if i % 2 else 3)
-    second = send(both, lambda i: 3 if i % 2 else 1)
+    late = send(both, lambda i: 3 if i % 2 else 1, lambda i: i == count // 2 - 3)
+    second = send(both, lambda i: 3 if i % 2 else 1, lambda i: i != count // 2 - 3)
     state = _own_call(me, doc_lengths, queries, both)
     first, state = lax.optimization_barrier((first, state))
+    first = jnp.concatenate(first, axis=1)
     chip = lax.all_gather(first, AXES, axis_index_groups=[[i, i + 1] for i in range(0, count, 2)])
-    blocks = (chip, second)
+    blocks = (chip, second, late)
     return tuple(_rest_call(me, doc_lengths, queries, blocks, state, both))
 
 

time: 62 us -> 61.6 us (level)
  starting transfers between devices: 6.23 us -> 10.6 us
  waiting for transfers between devices: 9.39 us -> 5.8 us
  blocking collectives: 3.57 us -> 2.69 us
    ppermute x2 -> x4, starting transfers between devices: 6.23 us -> 10.6 us  [send(): return lax.ppermute(block, AXES, pairs)]
    ppermute x2 -> x4, waiting for transfers between devices: 9.39 us -> 5.8 us  [send(): return lax.ppermute(block, AXES, pairs)]
    all_gather x1, blocking collectives: 3.57 us -> 2.69 us  [shards(): lax.all_gather(first, AXES, axis_index_groups=[[i, i + 1] for i in range(...]
  transfers between devices with their start and end apart: 2 -> 4, of which waited for: 1 -> 3; matrix products, arithmetic and copies ran while one was open for 0% -> 0% of each run, Pallas kernels for 4% -> 6%
where the time goes in v4:
time: 61.6 us; the launch traced here: 61.3 us
  Pallas kernels  39.6 us (64%)
  starting transfers between devices  10.6 us (17%)
  waiting for transfers between devices  5.8 us (9%)
  blocking collectives  2.69 us (4%)
  local copies, waits for them, and re-layouts  1.88 us (3%)
  between operations  0.69 us (1%)
    pallas_call x1, Pallas kernels, _rest_call(): pl.pallas_call(_rest, in_specs=[SCALARS, SCALARS, VMEM, ANYWHERE, ANYWHER...  36.1 us
    ppermute x4, starting transfers between devices, send(): return lax.ppermute(block, AXES, pairs)  10.6 us
    ppermute x4, waiting for transfers between devices, send(): return lax.ppermute(block, AXES, pairs)  5.8 us
    all_gather x1, blocking collectives, shards(): lax.all_gather(first, AXES, axis_index_groups=[[i, i + 1] for i in range(...  2.69 us
    pallas_call x1, Pallas kernels, _own_call(): pl.pallas_call(_own, in_specs=[SCALARS, SCALARS, VMEM, VMEM], out_specs=[...  2.55 us
    unnamed x4, local copies, waits for them, and re-layouts  1.88 us
  transfers between devices with their start and end apart: 4, of which 3 were waited for; matrix products, arithmetic and copies ran while one was open for 0% of the time, Pallas kernels for 6%

profile of v4, /device:TPU:8, one launch (start us, length us, event | category | flops | bytes accessed | tf_op | source)
XLA Modules:
  0.0 61.3 jit_solution(13660153323087440005)
XLA Ops:
  0.6 3.6 %collective-permute-start = (bf16[512,128]{1,0:T(8,128)(2,1)}, bf16[512,128]{1,0:T(8,128)(2,1)S(1)}, u32[]{:S(2)}, u32[]{:S(2)}) collective-permute-start(bf16[512,128]{1,0:T(8,128)(2,1)} %k.1), channel_id=1, source_target_pairs={{0,3},{1,2},{2,5},{3,4},{4,7},{5,6},{6,9},{7,8},{8,11},{9,10},{10,... | collective-permute-start | bytes 393224 | tf_op jit(solution)/shard_map/ppermute | solution.py:300
  4.3 4.4 %collective-permute-start.1 = (bf16[512,128]{1,0:T(8,128)(2,1)}, bf16[512,128]{1,0:T(8,128)(2,1)S(1)}, u32[]{:S(2)}, u32[]{:S(2)}) collective-permute-start(bf16[512,128]{1,0:T(8,128)(2,1)} %v.1), channel_id=1, source_target_pairs={{0,3},{1,2},{2,5},{3,4},{4,7},{5,6},{6,9},{7,8},{8,11},{9,10},{10,... | collective-permute-start | bytes 393224 | tf_op jit(solution)/shard_map/ppermute | solution.py:300
  8.6 1.0 %join.1.both = bf16[512,256]{1,0:T(8,128)(2,1)S(1)} custom-call(bf16[512,128]{1,0:T(8,128)(2,1)} %k.1, bf16[512,128]{1,0:T(8,128)(2,1)} %v.1), custom_call_target="tpu_custom_call" | custom-call | bytes 524288 | tf_op jit(solution)/shard_map/join/pallas_call | solution.py:230
  9.6 1.3 %collective-permute-start.3 = (bf16[512,256]{1,0:T(8,128)(2,1)S(1)}, bf16[512,256]{1,0:T(8,128)(2,1)S(1)}, u32[]{:S(2)}, u32[]{:S(2)}) collective-permute-start(bf16[512,256]{1,0:T(8,128)(2,1)S(1)} %join.1.both), channel_id=1, source_target_pairs={{253,256}} | collective-permute-start | bytes 786440 | tf_op jit(solution)/shard_map/ppermute | solution.py:300
  10.9 1.3 %collective-permute-start.2 = (bf16[512,256]{1,0:T(8,128)(2,1)S(1)}, bf16[512,256]{1,0:T(8,128)(2,1)S(1)}, u32[]{:S(2)}, u32[]{:S(2)}) collective-permute-start(bf16[512,256]{1,0:T(8,128)(2,1)S(1)} %join.1.both), channel_id=1, source_target_pairs={{0,1},{1,4},{2,3},{3,6},{4,5},{5,8},{6,7},{7,10},{8,9},{9,12},{10,... | collective-permute-start | bytes 786440 | tf_op jit(solution)/shard_map/ppermute | solution.py:300
  12.3 0.1 pad_add_fusion.me
  12.3 0.0 copy-start
  12.3 1.2 %copy-done = bf16[512,1024]{1,0:T(8,128)(2,1)S(1)} copy-done((bf16[512,1024]{1,0:T(8,128)(2,1)S(1)}, bf16[512,1024]{1,0:T(8,128)(2,1)}, u32[]{:S(2)}) %copy-start) | copy-done | bytes 1048600
  13.6 0.0 copy-start.1
  13.6 0.7 %copy-done.1 = s32[64]{0:T(128)S(1)} copy-done((s32[64]{0:T(128)S(1)}, s32[64]{0:T(128)}, u32[]{:S(2)}) %copy-start.1) | copy-done | bytes 280
  14.2 2.6 %own.1 = (f32[512,1024]{1,0:T(8,128)S(1)}, f32[512,128]{1,0:T(8,128)S(1)}, bf16[2048,128]{1,0:T(8,128)(2,1)S(1)}) custom-call(s32[2]{0:T(128)S(1)} %pad_add_fusion.me, s32[64]{0:T(128)S(1)} %copy-done.1, bf16[512,1024]{1,0:T(8,128)(2,1)S(1)} %copy-done, bf16[512,256]{1,0:T(8,128)(2,1)S(1)} %join.1.both), custom_call_target="tpu_custom_call" | custom-call | flops 671088640 | bytes 3145728 | tf_op jit(solution)/shard_map/own/pallas_call | solution.py:245
  16.8 1.3 %collective-permute-done = bf16[512,128]{1,0:T(8,128)(2,1)S(1)} collective-permute-done((bf16[512,128]{1,0:T(8,128)(2,1)}, bf16[512,128]{1,0:T(8,128)(2,1)S(1)}, u32[]{:S(2)}, u32[]{:S(2)}) %collective-permute-start) | collective-permute-done | bytes 131104 | tf_op jit(solution)/shard_map/ppermute | solution.py:300
  18.1 2.8 %collective-permute-done.1 = bf16[512,128]{1,0:T(8,128)(2,1)S(1)} collective-permute-done((bf16[512,128]{1,0:T(8,128)(2,1)}, bf16[512,128]{1,0:T(8,128)(2,1)S(1)}, u32[]{:S(2)}, u32[]{:S(2)}) %collective-permute-start.1) | collective-permute-done | bytes 131104 | tf_op jit(solution)/shard_map/ppermute | solution.py:300
  20.9 2.7 %all-gather = bf16[1024,256]{1,0:T(8,128)(2,1)S(1)} all-gather(bf16[512,256]{1,0:T(8,128)(2,1)S(1)} %pad_maximum_fusion), channel_id=2, replica_groups={{0,1},{2,3},{4,5},{6,7},{8,9},{10,11},{12,13},{14,15},{16,17},{18,19},{..., dimensions={0}, use_global_device_ids=true | all-gather | bytes 786432 | tf_op jit(solution)/shard_map/all_gather | solution.py:309
  23.6 1.7 %collective-permute-done.3.late = bf16[512,256]{1,0:T(8,128)(2,1)S(1)} collective-permute-done((bf16[512,256]{1,0:T(8,128)(2,1)S(1)}, bf16[512,256]{1,0:T(8,128)(2,1)S(1)}, u32[]{:S(2)}, u32[]{:S(2)}) %collective-permute-start.3) | collective-permute-done | bytes 262176 | tf_op jit(solution)/shard_map/ppermute | solution.py:300
  25.3 0.0 collective-permute-done.2.second
  25.3 36.1 %rest.1 = (bf16[512,1024]{1,0:T(8,128)(2,1)}, f32[8,512]{1,0:T(8,128)}) custom-call(s32[2]{0:T(128)S(1)} %pad_add_fusion.me, s32[64]{0:T(128)S(1)} %copy-done.1, bf16[512,1024]{1,0:T(8,128)(2,1)S(1)} %copy-done, bf16[2,512,256]{2,1,0:T(8,128)(2,1)S(1)} %bitcast.2, bf16[512,256]{1,0:T(8,128)(2,1)S(1)} %collective-permute-done.2.second, ...), custom_call_target="tpu_custom_call" | custom-call | flops 2818572288 | bytes 4194304 | tf_op jit(solution)/shard_map/rest/pallas_call | solution.py:268
  (1 shorter events, 0.0 us)
Async XLA Ops:
  0.6 17.5 %collective-permute-start = (bf16[512,128]{1,0:T(8,128)(2,1)}, bf16[512,128]{1,0:T(8,128)(2,1)S(1)}, u32[]{:S(2)}, u32[]{:S(2)}) collective-permute-start(bf16[512,128]{1,0:T(8,128)(2,1)} %k.1), channel_id=1, source_target_pairs={{0,3},{1,2},{2,5},{3,4},{4,7},{5,6},{6,9},{7,8},{8,11},{9,10},{10,... | collective-permute-start | bytes 393224 | tf_op jit(solution)/shard_map/ppermute | solution.py:300
  4.3 16.6 %collective-permute-start.1 = (bf16[512,128]{1,0:T(8,128)(2,1)}, bf16[512,128]{1,0:T(8,128)(2,1)S(1)}, u32[]{:S(2)}, u32[]{:S(2)}) collective-permute-start(bf16[512,128]{1,0:T(8,128)(2,1)} %v.1), channel_id=1, source_target_pairs={{0,3},{1,2},{2,5},{3,4},{4,7},{5,6},{6,9},{7,8},{8,11},{9,10},{10,... | collective-permute-start | bytes 393224 | tf_op jit(solution)/shard_map/ppermute | solution.py:300
  9.6 15.7 %collective-permute-start.3 = (bf16[512,256]{1,0:T(8,128)(2,1)S(1)}, bf16[512,256]{1,0:T(8,128)(2,1)S(1)}, u32[]{:S(2)}, u32[]{:S(2)}) collective-permute-start(bf16[512,256]{1,0:T(8,128)(2,1)S(1)} %join.1.both), channel_id=1, source_target_pairs={{253,256}} | collective-permute-start | bytes 786440 | tf_op jit(solution)/shard_map/ppermute | solution.py:300
  10.9 14.4 %collective-permute-start.2 = (bf16[512,256]{1,0:T(8,128)(2,1)S(1)}, bf16[512,256]{1,0:T(8,128)(2,1)S(1)}, u32[]{:S(2)}, u32[]{:S(2)}) collective-permute-start(bf16[512,256]{1,0:T(8,128)(2,1)S(1)} %join.1.both), channel_id=1, source_target_pairs={{0,1},{1,4},{2,3},{3,6},{4,5},{5,8},{6,7},{7,10},{8,9},{9,12},{10,... | collective-permute-start | bytes 786440 | tf_op jit(solution)/shard_map/ppermute | solution.py:300
  12.3 1.2 %copy-start = (bf16[512,1024]{1,0:T(8,128)(2,1)S(1)}, bf16[512,1024]{1,0:T(8,128)(2,1)}, u32[]{:S(2)}) copy-start(bf16[512,1024]{1,0:T(8,128)(2,1)} %q.3) | copy-start | bytes 3145732
  13.6 0.7 %copy-start.1 = (s32[64]{0:T(128)S(1)}, s32[64]{0:T(128)}, u32[]{:S(2)}) copy-start(s32[64]{0:T(128)} %lengths.3) | copy-start | bytes 772
